TPU v7x, 256 devices: a whole 4x4x8 slice. The times are simulated.
256 devices in a mesh: row: 16 (over y, z_lo), col: 16 (over x, z_hi, core).
Axes of the slice: x: 4, y: 4, z: 8 (z_hi: 2, z_lo: 4; z = z_hi * 4 + z_lo), core: 2. Of those that a mesh axis runs over, the one named last changes fastest.
Arguments:
- node_features: bfloat16 [16, 2048, 512], P('col', 'row'), may hold values from -6 to 6
- tile_coords: int32 [16, 16, 2, 128], P('row', 'col'), may hold values from 0 to 15, as said below
- tile_count: int32 [16, 16], P('row', 'col'), may hold values from 32 to 128, as said below
- tile_values: bfloat16 [16, 16, 128, 128, 128], P('row', 'col'), may hold values from -0.25 to 0.25
- weight: bfloat16 [512, 512], replicated, may hold values from -0.25 to 0.25
- cotangent: bfloat16 [16, 2048, 512], P('row', 'col'), may hold values from -6 to 6
Outputs:
- hidden: bfloat16 [16, 2048, 512], P('row', 'col')
- weight_grad: float32 [512, 512], replicated
- feature_grad: bfloat16 [16, 2048, 512], P('col', 'row')
Inputs may be any that keep to these rules, and one draw needn't show every extreme that they name: In each block (i, j), slot k names tile row tile_coords[i, j, 0, k] below 16 and tile column tile_coords[i, j, 1, k] below 16; the 128 pairs of a block are distinct. `tile_count`: the number of used slots of each block; some block uses all 128.
All inputs are finite; a program needn't handle non-finite values.
Results may differ from a plain program's by a relative error of at most 0.028.
Values may be sent and summed in bfloat16 or wider, within the bound.
No kernel may reach another device: no remote copies, remote signals or barrier semaphores. Data moves between devices by JAX's collectives and lax.ppermute only.
A program may use at most 128 MiB of HBM per device.

v0:
```python
import functools
import math

import jax
import jax.numpy as jnp
from jax import lax
from jax.experimental import pallas as pl
from jax.experimental.pallas import tpu as pltpu
from jax.sharding import PartitionSpec as P

Y = 4
Z = 4
X = 4
H = 2
C = 2
TILE = 128
VMEM_LIMIT = 4 * 1024 * 1024
STEP = 256
BF16 = jnp.bfloat16
F32 = jnp.float32


def row_shift(data, axis, step):
    pairs = []
    for r in range(Y * Z):
        y, z = divmod(r, Z)
        if axis == "y":
            source = (y + step) % Y * Z + z
        else:
            source = y * Z + (z + step) % Z
        pairs.append((source, r))
    return lax.ppermute(data, "row", pairs)


def col_shift(data, axis, step):
    pairs = []
    for c in range(X * H * C):
        x, h, k = c // (H * C), c // C % H, c % C
        if axis == "x":
            x = (x + step) % X
        elif axis == "h":
            h = (h + step) % H
        else:
            k = (k + step) % C
        pairs.append(((x * H + h) * C + k, c))
    return lax.ppermute(data, "col", pairs)


def densify_kernel(
    firsts, place_ref, count_ref, values_ref, *refs
):
    *dense_refs, held_ref, sems = refs
    size = dense_refs[0].shape[0]
    part = held_ref.shape[1]
    parts = values_ref.shape[0] // part

    def copy(i):
        return pltpu.make_async_copy(
            values_ref.at[pl.ds(i * part, part)], held_ref.at[i & 1], sems.at[i & 1]
        )

    copy(0).start()

    def clear(i, _):
        rows = pl.ds(pl.multiple_of(i * TILE, TILE), TILE)
        for ref in dense_refs:
            ref[rows, :] = jnp.zeros((TILE, ref.shape[1]), ref.dtype)
        return 0

    lax.fori_loop(0, size // TILE, clear, 0)

    def place_part(i, _):
        @pl.when(i + 1 < parts)
        def _():
            copy(i + 1).start()

        copy(i).wait()

        def put(k, _):
            r, c = place_ref[0, i * part + k], place_ref[1, i * part + k]
            for first, ref in zip(firsts, dense_refs):

                @pl.when((c >= first) & (c < first + ref.shape[1] // TILE))
                def _():
                    rows = pl.ds(pl.multiple_of(r * TILE, TILE), TILE)
                    columns = pl.ds(pl.multiple_of((c - first) * TILE, TILE), TILE)
                    ref[rows, columns] = held_ref[i & 1, k]

            return 0

        lax.fori_loop(0, jnp.clip(count_ref[0] - i * part, 0, part), put, 0)
        return 0

    lax.fori_loop(0, parts, place_part, 0)


def densify(values, place, count, *parts):
    size = 16 * TILE
    vmem = pl.BlockSpec(memory_space=pltpu.VMEM)
    return pl.pallas_call(
        functools.partial(densify_kernel, [first for first, _ in parts]),
        out_shape=[
            jax.ShapeDtypeStruct((size, (last - first) * TILE), values.dtype)
            for first, last in parts
        ],
        in_specs=[
            pl.BlockSpec(memory_space=pltpu.SMEM),
            pl.BlockSpec(memory_space=pltpu.SMEM),
            pl.BlockSpec(memory_space=pltpu.HBM),
        ],
        out_specs=[vmem] * len(parts),
        scratch_shapes=[
            pltpu.VMEM((2, 16, TILE, TILE), values.dtype),
            pltpu.SemaphoreType.DMA((2,)),
        ],
        compiler_params=pltpu.CompilerParams(vmem_limit_bytes=VMEM_LIMIT),
        cost_estimate=pl.CostEstimate(
            flops=0, bytes_accessed=12 * 1024 * 1024, transcendentals=0
        ),
    )(place, count, values)


def products_kernel(size, pieces, has_added, dense_ref, source_ref, *refs):
    outs = refs[1:] if has_added else refs
    for (first, last, _), out_ref in zip(pieces, outs):

        def step(i, _):
            start = pl.multiple_of(i * size, size)
            span = pl.ds(first * TILE + start, size)
            total = jnp.dot(
                dense_ref[span, :], source_ref[...], preferred_element_type=jnp.float32
            )
            if has_added:
                total += refs[0][span, :]
            out_ref[pl.ds(start, size), :] = total.astype(out_ref.dtype)
            return 0

        lax.fori_loop(0, (last - first) * TILE // size, step, 0)


def products(dense, source, added, size, pieces):
    width = source.shape[1]
    operands = [dense, source] + ([] if added is None else [added])
    vmem = pl.BlockSpec(memory_space=pltpu.VMEM)
    tiles = sum(last - first for first, last, _ in pieces)
    return pl.pallas_call(
        functools.partial(products_kernel, size, pieces, added is not None),
        out_shape=[
            jax.ShapeDtypeStruct(((last - first) * TILE, width), dtype)
            for first, last, dtype in pieces
        ],
        in_specs=[vmem] * len(operands),
        out_specs=[vmem] * len(pieces),
        compiler_params=pltpu.CompilerParams(vmem_limit_bytes=VMEM_LIMIT),
        cost_estimate=pl.CostEstimate(
            flops=2 * tiles * TILE * width * dense.shape[1],
            bytes_accessed=tiles * TILE * (dense.shape[1] + width) * 4,
            transcendentals=0,
        ),
    )(*operands)


def f32(value):
    return value.astype(jnp.float32)


def bf16(value):
    return value.astype(jnp.bfloat16)


def matmul(a, b):
    return jnp.dot(a, b, preferred_element_type=jnp.float32)


def join(*values):
    return lax.optimization_barrier(values)


def from_z(data):
    return [row_shift(data, "z", s) for s in (1, 2, 3)]


def from_y(data):
    return [row_shift(data, "y", s) for s in (1, 2, 3)]


def from_x(data):
    return [col_shift(data, "x", s) for s in (1, 2, 3)]


def rows_of(data, first, last):
    return data[first * TILE : last * TILE]


def total_of(own, parts):
    total = f32(own)
    for part in parts:
        total += f32(part)
    return total


def cut(value, index, size):
    return lax.dynamic_slice_in_dim(value, index * size, size, 0)


def call(kernel, outs, *operands, scratch=(), scalars=0, flops=0):
    vmem = pl.BlockSpec(memory_space=pltpu.VMEM)
    shapes = [jax.ShapeDtypeStruct(shape, dtype) for shape, dtype in outs]
    return pl.pallas_call(
        kernel,
        out_shape=shapes,
        in_specs=[pl.BlockSpec(memory_space=pltpu.SMEM)] * scalars
        + [vmem] * (len(operands) - scalars),
        out_specs=[vmem] * len(outs),
        scratch_shapes=list(scratch),
        compiler_params=pltpu.CompilerParams(vmem_limit_bytes=VMEM_LIMIT),
        cost_estimate=pl.CostEstimate(
            flops=flops, bytes_accessed=4 * 1024 * 1024, transcendentals=0
        ),
    )(*operands)


def split_for_x(me_x, both_ref, outs):
    full = both_ref.shape[0] // 2
    for s, ref in enumerate(outs):
        first = pl.multiple_of(full + ((me_x - s) & 3) * TILE, TILE)
        ref[:full, :] = both_ref[:full, :]
        ref[full:, :] = both_ref[pl.ds(first, TILE), :]


def middle_kernel(
    me_ref, own_ref, p0, p1, p2, p3, weight_ref, cotangent_ref, hidden_ref, both_ref, *outs
):
    full = weight_ref.shape[0]
    total = own_ref[...] + f32(p0[...]) + f32(p1[...]) + f32(p2[...]) + f32(p3[...])
    summed = bf16(total)
    both_ref[full:, :] = summed.T
    pre = matmul(summed, weight_ref[...])
    sigma = 1.0 / (1.0 + jnp.exp(-pre))
    hidden_ref[...] = bf16(pre * sigma)
    slope = sigma * (1.0 + pre * (1.0 - sigma))
    both_ref[:full, :] = bf16(f32(cotangent_ref[...]) * slope).T
    split_for_x(me_ref[0], both_ref, outs)


def split_kernel(me_ref, both_ref, *outs):
    split_for_x(me_ref[0], both_ref, outs)


def first_kernel(dense1_ref, dense2_ref, source_ref, near_ref, far_ref):
    nodes = source_ref.shape[1]
    for dense_ref, ref in ((dense1_ref, near_ref), (dense2_ref, far_ref)):

        def step(i, _):
            here = pl.ds(pl.multiple_of(i * TILE, TILE), TILE)
            ref[here, :] = matmul(source_ref[here, :], dense_ref[:nodes, :])
            return 0

        lax.fori_loop(0, ref.shape[0] // TILE, step, 0)


def lead_kernel(me_ref, dense_ref, source_ref, first_ref, added_ref, *refs):
    lead1, over1, lead2, over3, lead3, w_ref, *totals = refs
    full, nodes = lead1.shape[0], source_ref.shape[1]
    for ref, total_ref in zip((first_ref, source_ref), totals):

        def step(i, _):
            here = pl.ds(pl.multiple_of(i * TILE, TILE), TILE)
            total_ref[:, here] = lax.dot_general(
                ref[full:, :],
                ref[here, :],
                (((1,), (1,)), ((), ())),
                preferred_element_type=jnp.float32,
            )
            return 0

        lax.fori_loop(0, full // TILE, step, 0)
    rows = w_ref.shape[0] * TILE // full
    span = pl.ds(pl.multiple_of(me_ref[1] * rows, rows), rows)
    w = bf16(totals[0][span, :] + totals[1][span, :])
    for i in range(full // TILE):
        w_ref[i * rows : (i + 1) * rows, :] = w[:, i * TILE : (i + 1) * TILE]

    def step(i, _):
        here = pl.ds(pl.multiple_of(i * STEP, STEP), STEP)
        total = bf16(matmul(source_ref[here, :], dense_ref[nodes:, :]) + added_ref[here, :])
        start = 0
        for ref in (lead1, over1, lead2, over3, lead3):
            ref[here, :] = total[:, start : start + ref.shape[1]]
            start += ref.shape[1]
        return 0

    lax.fori_loop(0, full // STEP, step, 0)
    for ref in (over1, over3):
        ref[full:, :] = w_ref[...]


def rest_kernel(dense_ref, source_ref, added_ref, across_ref, w0_ref, w2_ref, *refs):
    near1, near2, near3, run, own, pair = refs
    full, nodes = own.shape[0], source_ref.shape[1]
    pair[...] = f32(w0_ref[...]) + f32(w2_ref[...])

    def step(i, _):
        here = pl.ds(pl.multiple_of(i * STEP, STEP), STEP)
        total = matmul(source_ref[here, :], dense_ref[nodes:, :]) + added_ref[here, :]
        start = 0
        for ref in (own, run, near1, near2, near3):
            ref[here, :] = total[:, start : start + ref.shape[1]].astype(ref.dtype)
            start += ref.shape[1]
        return 0

    lax.fori_loop(0, full // STEP, step, 0)
    run[:, TILE : 2 * TILE] += f32(across_ref[...])


def combine_kernel(
    run, near1, near2, near3, pair, down, up, over1, over3, z1, z2, z3, y1, y2, y3, w_out
):
    full = run.shape[0]
    for s, ref in enumerate((z1, z2, z3)):
        span = slice(s * TILE, (s + 1) * TILE)
        ref[...] = bf16(run[:, span] + f32(down[:, span]) + f32(up[:, span]))
    y1[:full, :] = near1[...]
    y2[:full, :] = bf16(near2[...] + f32(over1[:full, :]) + f32(over3[:full, :]))
    y3[:full, :] = near3[...]
    total = bf16(pair[...] + (f32(over1[full:, :]) + f32(over3[full:, :])))
    for ref in (y1, y2, y3):
        ref[full:, :] = total
    w_out[...] = total


def sum_of_four(parts):
    return (f32(parts[0]) + f32(parts[2])) + (f32(parts[1]) + f32(parts[3]))


def assemble_kernel(me_ref, own_ref, other_ref, out_ref):
    parts = out_ref.shape[1] // TILE
    rows = own_ref.shape[0] // X // parts
    for s in range(X):
        first = (me_ref[0] + s & 3) * C * rows
        for ref, core in ((own_ref, me_ref[1]), (other_ref, 1 - me_ref[1])):
            place = pl.ds(pl.multiple_of(first + core * rows, rows), rows)
            for i in range(parts):
                start = (s * parts + i) * rows
                out_ref[place, i * TILE : (i + 1) * TILE] = ref[start : start + rows, :]


def body(node_features, tile_coords, tile_count, tile_values, weight, cotangent):
    features = node_features[0]
    me_row = lax.axis_index("row")
    me_col = lax.axis_index("col")
    my, mz = me_row >> 2, me_row & 3
    mx, mh, mk = me_col >> 2, me_col >> 1 & 1, me_col & 1
    nodes_all = TILE * Y * Z * X * H * C
    full = features.shape[1]

    tr, tc = tile_coords[0, 0, 0], tile_coords[0, 0, 1]
    place_r = ((tr >> 1) + mh & 1) * 8 + (tr + mk & 1) * 4 + ((tr >> 2) - mx & 3)
    far_y, far_z = (tc >> 2) - my & 3, tc - mz & 3
    place_c = jnp.where(
        far_y == 0, far_z, jnp.where(far_z == 0, 3 + far_y, 3 + far_y * 3 + far_z)
    )
    place = jnp.stack([place_r, place_c])
    values, count = tile_values[0, 0], tile_count[0]

    along_y = from_y(features)
    along_z, along_y[1], forward = join(
        from_z(features), along_y[1], densify(values, place, count, (0, 7), (7, 16))
    )
    rest = jnp.concatenate(along_z)
    near = jnp.concatenate([features, rest] + along_y)
    far = [row_shift(rest, "y", 1), row_shift(rest, "y", 3)]
    far += [row_shift(along_y[1], "z", 1), row_shift(along_y[1], "z", 3)]
    far += [row_shift(along_z[1], "y", 2)]
    far, near = join(far, products(forward[0], near, None, TILE, [(0, 16, F32)])[0])
    far = jnp.concatenate([far[0], far[2], far[4], far[3], far[1]])

    (away,) = products(forward[1], far, near, 512, [(12, 16, BF16)])
    away, far = join(away, far)
    arrived = col_shift(away, "k", 1)
    (rest,) = products(forward[1], far, near, 512, [(0, 12, F32)])
    home, away, own = rows_of(rest, 8, 12), bf16(rows_of(rest, 4, 8)), rows_of(rest, 0, 4)
    home, arrived, away, own = join(home, arrived, away, own)
    lead = [bf16(rows_of(home, s, s + 1) + f32(rows_of(arrived, s, s + 1))) for s in range(X)]
    lead_parts = [col_shift(lead[s], "x", X - s) for s in (1, 2, 3)]
    lead, arrived = lead[0], col_shift(away, "k", 1)
    lead = bf16(total_of(lead, lead_parts))
    own = [rows_of(own, s, s + 1) + f32(rows_of(arrived, s, s + 1)) for s in range(X)]
    lead = col_shift(lead, "h", 1)
    own_parts = [col_shift(bf16(own[s]), "x", X - s) for s in (1, 2, 3)]
    me = jnp.stack([mx, mk])
    wider = full + TILE
    hidden, both, *own_sent = call(
        middle_kernel,
        [((TILE, full), BF16), ((2 * full, TILE), BF16)] + [((wider, TILE), BF16)] * X,
        me,
        own[0],
        lead,
        *own_parts,
        weight,
        cotangent[0],
        scalars=1,
        flops=2 * TILE * full * full,
    )

    other = col_shift(both, "h", 1)
    own_parts = [col_shift(own_sent[s], "x", s) for s in (1, 2, 3)]
    other, own_parts = join(other, own_parts)
    own = jnp.concatenate([own_sent[0]] + own_parts, axis=1)
    other_sent = call(split_kernel, [((wider, TILE), BF16)] * X, me, other, scalars=1)
    own_core = col_shift(own, "k", 1)
    other_parts = [col_shift(other_sent[s], "x", s) for s in (1, 2, 3)]
    first = jnp.concatenate([own, own_core], axis=1)
    near, far = call(
        first_kernel,
        [((full, 7 * TILE), F32), ((full, 9 * TILE), F32)],
        *forward,
        first,
        flops=2 * 16 * TILE * full * 8 * TILE,
    )
    other_parts, near, far, first = join(other_parts, near, far, first)
    other = jnp.concatenate([other_sent[0]] + other_parts, axis=1)
    source = jnp.concatenate([other, col_shift(other, "k", 1)], axis=1)

    rows = full * full // (X * C) // TILE
    lead1, over1, lead2, over3, lead3, w = call(
        lead_kernel,
        [((full, 3 * TILE), BF16), ((full + rows, TILE), BF16), ((full, TILE), BF16)]
        + [((full + rows, TILE), BF16), ((full, 3 * TILE), BF16), ((rows, TILE), BF16)],
        me,
        forward[1],
        source,
        first,
        far,
        scratch=[pltpu.VMEM((TILE, full), F32)] * 2,
        scalars=1,
        flops=2 * 9 * TILE * full * 8 * TILE,
    )
    near1, near2, near3, run, own, pair = call(
        rest_kernel,
        [((full, TILE), BF16), ((full, TILE), F32), ((full, TILE), BF16)]
        + [((full, 3 * TILE), F32), ((full, TILE), F32), ((rows, TILE), F32)],
        forward[0],
        source,
        near,
        row_shift(lead2, "y", 2),
        w,
        row_shift(w, "z", 2),
        flops=2 * 7 * TILE * full * 8 * TILE,
    )
    parts = join(
        row_shift(lead1, "y", 3),
        row_shift(lead3, "y", 1),
        row_shift(over1, "z", 3),
        row_shift(over3, "z", 1),
    )
    *run, near1, near2, near3, w = call(
        combine_kernel,
        [((full, TILE), BF16)] * 3 + [((full + rows, TILE), BF16)] * 3 + [((rows, TILE), BF16)],
        run,
        near1,
        near2,
        near3,
        pair,
        *parts,
    )
    z_parts = [row_shift(run[s - 1], "z", Z - s) for s in (1, 2, 3)]
    near_parts = [
        row_shift(near, "y", Y - s) for s, near in ((1, near1), (2, near2), (3, near3))
    ]
    z_parts, near_parts = join(z_parts, near_parts)
    w = bf16(sum_of_four([w] + [part[full:] for part in near_parts]))
    (w,) = join(w)
    w_parts = from_x(w)
    back = bf16(total_of(own, [part[:full] for part in near_parts] + z_parts))
    feature_grad = bf16(
        lax.dot_general(
            back, weight, (((0,), (1,)), ((), ())), preferred_element_type=jnp.float32
        )
    )

    parts = jnp.concatenate([w] + w_parts)
    (w,) = call(
        assemble_kernel, [((full, full), BF16)], me, parts, col_shift(parts, "k", 1), scalars=1
    )
    weight_grad = f32(w) / math.sqrt(nodes_all)
    return (hidden[None], weight_grad, feature_grad[None])


def solution(mesh):
    in_specs = (
        P("col", "row", None),
        P("row", "col", None, None),
        P("row", "col"),
        P("row", "col", None, None, None),
        P(),
        P("row", "col", None),
    )
    out_specs = (P("row", "col", None), P(), P("col", "row", None))
    return jax.shard_map(body, mesh=mesh, in_specs=in_specs, out_specs=out_specs, check_vma=False)
```

profile of v0, /device:TPU:6, one launch (start us, length us, event | category | flops | bytes accessed | tf_op | source)
XLA Modules:
  0.0 145.5 jit_solution(13234517190530273909)
XLA Ops:
  0.6 1.7 %collective-permute-start.10 = (bf16[128,512]{1,0:T(8,128)(2,1)}, bf16[128,512]{1,0:T(8,128)(2,1)S(1)}, u32[]{:S(2)}, u32[]{:S(2)}) collective-permute-start(bf16[128,512]{1,0:T(8,128)(2,1)} %bitcast.26), channel_id=1, source_target_pairs={{192,0},{208,16},{224,32},{240,48},{0,64},{16,80},{32,96},{48,112}... | collective-permute-start | bytes 393224 | tf_op jit(solution)/shard_map/ppermute | solution.py:32
  2.3 2.9 %collective-permute-start.3 = (bf16[128,512]{1,0:T(8,128)(2,1)}, bf16[128,512]{1,0:T(8,128)(2,1)S(1)}, u32[]{:S(2)}, u32[]{:S(2)}) collective-permute-start(bf16[128,512]{1,0:T(8,128)(2,1)} %bitcast.27), channel_id=1, source_target_pairs={{128,0},{144,16},{160,32},{176,48},{192,64},{208,80},{224,96},{240... | collective-permute-start | bytes 393224 | tf_op jit(solution)/shard_map/ppermute | solution.py:32
  5.2 1.9 %collective-permute-start.2 = (bf16[128,512]{1,0:T(8,128)(2,1)}, bf16[128,512]{1,0:T(8,128)(2,1)S(1)}, u32[]{:S(2)}, u32[]{:S(2)}) collective-permute-start(bf16[128,512]{1,0:T(8,128)(2,1)} %bitcast.28), channel_id=1, source_target_pairs={{48,0},{0,16},{16,32},{32,48},{112,64},{64,80},{80,96},{96,112},{1... | collective-permute-start | bytes 393224 | tf_op jit(solution)/shard_map/ppermute | solution.py:32
  7.1 3.3 %collective-permute-start.1 = (bf16[128,512]{1,0:T(8,128)(2,1)}, bf16[128,512]{1,0:T(8,128)(2,1)S(1)}, u32[]{:S(2)}, u32[]{:S(2)}) collective-permute-start(bf16[128,512]{1,0:T(8,128)(2,1)} %bitcast.29), channel_id=1, source_target_pairs={{32,0},{48,16},{0,32},{16,48},{96,64},{112,80},{64,96},{80,112},{1... | collective-permute-start | bytes 393224 | tf_op jit(solution)/shard_map/ppermute | solution.py:32
  10.4 1.0 collective-permute-start
  12.0 0.7 bitcast_select_fusion
  12.7 0.7 add_bitcast_fusion
  13.4 2.2 %copy-done = bf16[1,1,128,128,128]{4,3,2,1,0:T(8,128)(2,1)S(1)} copy-done((bf16[1,1,128,128,128]{4,3,2,1,0:T(8,128)(2,1)S(1)}, bf16[1,1,128,128,128]{4,3,2,1,0:T(8,128)(2,1)}, u32[]{:S(2)}) %copy-start) | copy-done | bytes 4194328
  15.6 4.2 %shard_map.85 = (bf16[2048,896]{1,0:T(8,128)(2,1)S(1)}, bf16[2048,1152]{1,0:T(8,128)(2,1)S(1)}) custom-call(s32[2,128]{1,0:T(2,128)S(1)} %pad_add_fusion.place_ref, s32[1]{0:T(128)} %bitcast.23.count_ref, bf16[128,128,128]{2,1,0:T(8,128)(2,1)S(1)} %bitcast.24), custom_call_target="tpu_custom_call" | custom-call | bytes 12582912 | tf_op jit(solution)/shard_map/pallas_call | solution.py:100
  19.8 1.0 collective-permute-start.9
  21.0 1.2 collective-permute-start.5
  22.2 2.7 %collective-permute-start.4 = (bf16[384,512]{1,0:T(8,128)(2,1)S(1)}, bf16[384,512]{1,0:T(8,128)(2,1)S(1)}, u32[]{:S(2)}, u32[]{:S(2)}) collective-permute-start(bf16[384,512]{1,0:T(8,128)(2,1)S(1)} %get-tuple-element.155), channel_id=1, source_target_pairs={{64,0},{80,16},{96,32},{112,48},{128,64},{144,80},{160,96},{176,11... | collective-permute-start | bytes 1179656 | tf_op jit(solution)/shard_map/ppermute | solution.py:32
  25.0 0.8 collective-permute-done.9
  26.3 3.4 %collective-permute-start.6 = (bf16[128,512]{1,0:T(8,128)(2,1)S(1)}, bf16[128,512]{1,0:T(8,128)(2,1)S(1)}, u32[]{:S(2)}, u32[]{:S(2)}) collective-permute-start(bf16[128,512]{1,0:T(8,128)(2,1)S(1)} %collective-permute-done.3), channel_id=1, source_target_pairs={{16,0},{32,16},{48,32},{0,48},{80,64},{96,80},{112,96},{64,112},{1... | collective-permute-start | bytes 393224 | tf_op jit(solution)/shard_map/ppermute | solution.py:32
  29.7 4.9 %shard_map.86.refs_0_ = f32[2048,512]{1,0:T(8,128)S(1)} custom-call(bf16[2048,896]{1,0:T(8,128)(2,1)S(1)} %get-tuple-element.81.dense_ref.dense1_ref, bf16[896,512]{1,0:T(8,128)(2,1)S(1)} %constant_dynamic-update-slice_fusion.3.source_ref), custom_call_target="tpu_custom_call" | custom-call | flops 1879048192 | bytes 11534336 | tf_op jit(solution)/shard_map/pallas_call | solution.py:146
  34.7 1.0 collective-permute-done.5
  35.7 0.8 shard_map.87
  36.7 2.5 %shard_map.88 = f32[1536,512]{1,0:T(8,128)S(1)} custom-call(bf16[2048,1152]{1,0:T(8,128)(2,1)S(1)} %get-tuple-element.76.dense_ref.dense2_ref, bf16[1152,512]{1,0:T(8,128)(2,1)S(1)} %constant_dynamic-update-slice_fusion.10.source_ref, f32[2048,512]{1,0:T(8,128)S(1)} %shard_map.86.refs_0_), custom_call_target="tpu_custom_call" | custom-call | flops 1811939328 | bytes 10223616 | tf_op jit(solution)/shard_map/pallas_call | solution.py:146
  39.5 0.6 collective-permute-start.12
  40.2 1.7 %collective-permute-start.13 = (bf16[128,512]{1,0:T(8,128)(2,1)S(1)}, bf16[128,512]{1,0:T(8,128)(2,1)S(1)}, u32[]{:S(2)}, u32[]{:S(2)}) collective-permute-start(bf16[128,512]{1,0:T(8,128)(2,1)S(1)} %get-tuple-element.151), channel_id=1, source_target_pairs={{12,0},{13,1},{14,2},{15,3},{0,4},{1,5},{2,6},{3,7},{4,8},{5,9},{6... | collective-permute-start | bytes 393224 | tf_op jit(solution)/shard_map/ppermute | solution.py:46
  42.3 1.8 %collective-permute-start.14 = (bf16[128,512]{1,0:T(8,128)(2,1)S(1)}, bf16[128,512]{1,0:T(8,128)(2,1)S(1)}, u32[]{:S(2)}, u32[]{:S(2)}) collective-permute-start(bf16[128,512]{1,0:T(8,128)(2,1)S(1)} %get-tuple-element.153), channel_id=1, source_target_pairs={{8,0},{9,1},{10,2},{11,3},{12,4},{13,5},{14,6},{15,7},{0,8},{1,9},... | collective-permute-start | bytes 393224 | tf_op jit(solution)/shard_map/ppermute | solution.py:46
  44.1 1.6 %collective-permute-done.13 = bf16[128,512]{1,0:T(8,128)(2,1)S(1)} collective-permute-done((bf16[128,512]{1,0:T(8,128)(2,1)S(1)}, bf16[128,512]{1,0:T(8,128)(2,1)S(1)}, u32[]{:S(2)}, u32[]{:S(2)}) %collective-permute-start.13) | collective-permute-done | bytes 131104 | tf_op jit(solution)/shard_map/ppermute | solution.py:46
  45.7 5.4 %collective-permute-done.15 = bf16[128,512]{1,0:T(8,128)(2,1)S(1)} collective-permute-done((bf16[128,512]{1,0:T(8,128)(2,1)S(1)}, bf16[128,512]{1,0:T(8,128)(2,1)S(1)}, u32[]{:S(2)}, u32[]{:S(2)}) %collective-permute-start.15) | collective-permute-done | bytes 131104 | tf_op jit(solution)/shard_map/ppermute | solution.py:46
  51.2 4.9 %collective-permute-start.16 = (bf16[128,512]{1,0:T(8,128)(2,1)S(1)}, bf16[128,512]{1,0:T(8,128)(2,1)S(1)}, u32[]{:S(2)}, u32[]{:S(2)}) collective-permute-start(bf16[128,512]{1,0:T(8,128)(2,1)S(1)} %add_convert_fusion.4), channel_id=1, source_target_pairs={{2,0},{3,1},{0,2},{1,3},{6,4},{7,5},{4,6},{5,7},{10,8},{11,9},{8,1... | collective-permute-start | bytes 393224 | tf_op jit(solution)/shard_map/ppermute | solution.py:46
  56.4 2.8 %collective-permute-start.18 = (bf16[128,512]{1,0:T(8,128)(2,1)S(1)}, bf16[128,512]{1,0:T(8,128)(2,1)S(1)}, u32[]{:S(2)}, u32[]{:S(2)}) collective-permute-start(bf16[128,512]{1,0:T(8,128)(2,1)S(1)} %get-tuple-element.148), channel_id=1, source_target_pairs={{8,0},{9,1},{10,2},{11,3},{12,4},{13,5},{14,6},{15,7},{0,8},{1,9},... | collective-permute-start | bytes 393224 | tf_op jit(solution)/shard_map/ppermute | solution.py:46
  59.2 1.7 %collective-permute-start.17 = (bf16[128,512]{1,0:T(8,128)(2,1)S(1)}, bf16[128,512]{1,0:T(8,128)(2,1)S(1)}, u32[]{:S(2)}, u32[]{:S(2)}) collective-permute-start(bf16[128,512]{1,0:T(8,128)(2,1)S(1)} %get-tuple-element.149), channel_id=1, source_target_pairs={{12,0},{13,1},{14,2},{15,3},{0,4},{1,5},{2,6},{3,7},{4,8},{5,9},{6... | collective-permute-start | bytes 393224 | tf_op jit(solution)/shard_map/ppermute | solution.py:46
  61.6 3.1 %collective-permute-done.19.p3 = bf16[128,512]{1,0:T(8,128)(2,1)S(1)} collective-permute-done((bf16[128,512]{1,0:T(8,128)(2,1)S(1)}, bf16[128,512]{1,0:T(8,128)(2,1)S(1)}, u32[]{:S(2)}, u32[]{:S(2)}) %collective-permute-start.19) | collective-permute-done | bytes 131104 | tf_op jit(solution)/shard_map/ppermute | solution.py:46
  65.3 1.5 %shard_map.89 = (bf16[128,512]{1,0:T(8,128)(2,1)}, bf16[1024,128]{1,0:T(8,128)(2,1)S(1)}, bf16[640,128]{1,0:T(8,128)(2,1)S(1)}, bf16[640,128]{1,0:T(8,128)(2,1)S...) custom-call(s32[2]{0:T(128)S(1)} %pad_add_fusion.1.me_ref, f32[128,512]{1,0:T(8,128)S(1)} %get-tuple-element.150.own_ref, ...), custom_call_target="tpu_custom_call" | custom-call | flops 67108864 | bytes 4194304 | tf_op jit(solution)/shard_map/pallas_call | solution.py:209
  66.8 1.2 collective-permute-start.20
  68.3 3.5 %collective-permute-start.22 = (bf16[640,128]{1,0:T(8,128)(2,1)S(1)}, bf16[640,128]{1,0:T(8,128)(2,1)S(1)}, u32[]{:S(2)}, u32[]{:S(2)}) collective-permute-start(bf16[640,128]{1,0:T(8,128)(2,1)S(1)} %get-tuple-element.97), channel_id=1, source_target_pairs={{8,0},{9,1},{10,2},{11,3},{12,4},{13,5},{14,6},{15,7},{0,8},{1,9},... | collective-permute-start | bytes 491528 | tf_op jit(solution)/shard_map/ppermute | solution.py:46
  72.1 3.0 %collective-permute-done.21 = bf16[640,128]{1,0:T(8,128)(2,1)S(1)} collective-permute-done((bf16[640,128]{1,0:T(8,128)(2,1)S(1)}, bf16[640,128]{1,0:T(8,128)(2,1)S(1)}, u32[]{:S(2)}, u32[]{:S(2)}) %collective-permute-start.21) | collective-permute-done | bytes 163872 | tf_op jit(solution)/shard_map/ppermute | solution.py:46
  75.1 1.8 %collective-permute-done.22 = bf16[640,128]{1,0:T(8,128)(2,1)S(1)} collective-permute-done((bf16[640,128]{1,0:T(8,128)(2,1)S(1)}, bf16[640,128]{1,0:T(8,128)(2,1)S(1)}, u32[]{:S(2)}, u32[]{:S(2)}) %collective-permute-start.22) | collective-permute-done | bytes 163872 | tf_op jit(solution)/shard_map/ppermute | solution.py:46
  77.2 1.5 %collective-permute-done.20.both_ref = bf16[1024,128]{1,0:T(8,128)(2,1)S(1)} collective-permute-done((bf16[1024,128]{1,0:T(8,128)(2,1)S(1)}, bf16[1024,128]{1,0:T(8,128)(2,1)S(1)}, u32[]{:S(2)}, u32[]{:S(2)}) %collective-permute-start.20) | collective-permute-done | bytes 262176 | tf_op jit(solution)/shard_map/ppermute | solution.py:46
  78.9 0.6 shard_map.90
  79.6 1.5 %collective-permute-start.24 = (bf16[640,128]{1,0:T(8,128)(2,1)S(1)}, bf16[640,128]{1,0:T(8,128)(2,1)S(1)}, u32[]{:S(2)}, u32[]{:S(2)}) collective-permute-start(bf16[640,128]{1,0:T(8,128)(2,1)S(1)} %get-tuple-element.101), channel_id=1, source_target_pairs={{4,0},{5,1},{6,2},{7,3},{8,4},{9,5},{10,6},{11,7},{12,8},{13,9},{1... | collective-permute-start | bytes 491528 | tf_op jit(solution)/shard_map/ppermute | solution.py:46
  81.1 3.6 %collective-permute-start.25 = (bf16[640,128]{1,0:T(8,128)(2,1)S(1)}, bf16[640,128]{1,0:T(8,128)(2,1)S(1)}, u32[]{:S(2)}, u32[]{:S(2)}) collective-permute-start(bf16[640,128]{1,0:T(8,128)(2,1)S(1)} %get-tuple-element.102), channel_id=1, source_target_pairs={{8,0},{9,1},{10,2},{11,3},{12,4},{13,5},{14,6},{15,7},{0,8},{1,9},... | collective-permute-start | bytes 491528 | tf_op jit(solution)/shard_map/ppermute | solution.py:46
  84.9 3.9 %shard_map.91 = (f32[512,896]{1,0:T(8,128)S(1)}, f32[512,1152]{1,0:T(8,128)S(1)}) custom-call(bf16[2048,896]{1,0:T(8,128)(2,1)S(1)} %get-tuple-element.81.dense_ref.dense1_ref, bf16[2048,1152]{1,0:T(8,128)(2,1)S(1)} %get-tuple-element.76.dense_ref.dense2_ref, bf16[640,1024]{1,0:T(8,128)(2,1)S(1)} %constant_dynamic-update-slice_fusion.15.source_ref.first_ref), custom_call_target="tpu_custom_call" | custom-call | flops 2147483648 | bytes 4194304 | tf_op jit(solution)/shard_map/pallas_call | solution.py:209
  88.8 3.9 %collective-permute-done.25 = bf16[640,128]{1,0:T(8,128)(2,1)S(1)} collective-permute-done((bf16[640,128]{1,0:T(8,128)(2,1)S(1)}, bf16[640,128]{1,0:T(8,128)(2,1)S(1)}, u32[]{:S(2)}, u32[]{:S(2)}) %collective-permute-start.25) | collective-permute-done | bytes 163872 | tf_op jit(solution)/shard_map/ppermute | solution.py:46
  93.1 1.9 %collective-permute-done.28 = bf16[640,512]{1,0:T(8,128)(2,1)S(1)} collective-permute-done((bf16[640,512]{1,0:T(8,128)(2,1)S(1)}, bf16[640,512]{1,0:T(8,128)(2,1)S(1)}, u32[]{:S(2)}, u32[]{:S(2)}) %collective-permute-start.28) | collective-permute-done | bytes 655392 | tf_op jit(solution)/shard_map/ppermute | solution.py:46
  95.1 4.2 %shard_map.92 = (bf16[512,384]{1,0:T(8,128)(2,1)S(1)}, bf16[768,128]{1,0:T(8,128)(2,1)S(1)}, bf16[512,128]{1,0:T(8,128)(2,1)S(1)}, bf16[768,128]{1,0:T(8,128)(2,...) custom-call(s32[2]{0:T(128)S(1)} %pad_add_fusion.1.me_ref, ...), custom_call_target="tpu_custom_call" | custom-call | flops 1207959552 | bytes 4194304 | tf_op jit(solution)/shard_map/pallas_call | solution.py:209
  99.3 1.2 collective-permute-start.31
  100.5 2.9 %collective-permute-start.32 = (bf16[512,384]{1,0:T(8,128)(2,1)S(1)}, bf16[512,384]{1,0:T(8,128)(2,1)S(1)}, u32[]{:S(2)}, u32[]{:S(2)}) collective-permute-start(bf16[512,384]{1,0:T(8,128)(2,1)S(1)} %get-tuple-element.124), channel_id=1, source_target_pairs={{64,0},{80,16},{96,32},{112,48},{128,64},{144,80},{160,96},{176,11... | collective-permute-start | bytes 1179656 | tf_op jit(solution)/shard_map/ppermute | solution.py:32
  103.4 1.8 %collective-permute-start.30 = (bf16[256,128]{1,0:T(8,128)(2,1)S(1)}, bf16[256,128]{1,0:T(8,128)(2,1)S(1)}, u32[]{:S(2)}, u32[]{:S(2)}) collective-permute-start(bf16[256,128]{1,0:T(8,128)(2,1)S(1)} %get-tuple-element.117.w0_ref), channel_id=1, source_target_pairs={{32,0},{48,16},{0,32},{16,48},{96,64},{112,80},{64,96},{80,112},{1... | collective-permute-start | bytes 196616 | tf_op jit(solution)/shard_map/ppermute | solution.py:32
  105.4 2.5 %collective-permute-start.33 = (bf16[768,128]{1,0:T(8,128)(2,1)S(1)}, bf16[768,128]{1,0:T(8,128)(2,1)S(1)}, u32[]{:S(2)}, u32[]{:S(2)}) collective-permute-start(bf16[768,128]{1,0:T(8,128)(2,1)S(1)} %get-tuple-element.125), channel_id=1, source_target_pairs={{48,0},{0,16},{16,32},{32,48},{112,64},{64,80},{80,96},{96,112},{1... | collective-permute-start | bytes 589832 | tf_op jit(solution)/shard_map/ppermute | solution.py:32
  107.8 0.7 collective-permute-done.30.w2_ref
  108.6 4.6 %collective-permute-start.34 = (bf16[768,128]{1,0:T(8,128)(2,1)S(1)}, bf16[768,128]{1,0:T(8,128)(2,1)S(1)}, u32[]{:S(2)}, u32[]{:S(2)}) collective-permute-start(bf16[768,128]{1,0:T(8,128)(2,1)S(1)} %get-tuple-element.126), channel_id=1, source_target_pairs={{16,0},{32,16},{48,32},{0,48},{80,64},{96,80},{112,96},{64,112},{1... | collective-permute-start | bytes 589832 | tf_op jit(solution)/shard_map/ppermute | solution.py:32
  113.2 3.5 %collective-permute-done.29.across_ref = bf16[512,128]{1,0:T(8,128)(2,1)S(1)} collective-permute-done((bf16[512,128]{1,0:T(8,128)(2,1)S(1)}, bf16[512,128]{1,0:T(8,128)(2,1)S(1)}, u32[]{:S(2)}, u32[]{:S(2)}) %collective-permute-start.29) | collective-permute-done | bytes 131104 | tf_op jit(solution)/shard_map/ppermute | solution.py:32
  116.7 1.5 shard_map.93
  118.4 0.8 collective-permute-start.35
  119.2 1.4 collective-permute-start.38
  120.6 2.3 %collective-permute-start.39 = (bf16[768,128]{1,0:T(8,128)(2,1)S(1)}, bf16[768,128]{1,0:T(8,128)(2,1)S(1)}, u32[]{:S(2)}, u32[]{:S(2)}) collective-permute-start(bf16[768,128]{1,0:T(8,128)(2,1)S(1)} %get-tuple-element.136), channel_id=1, source_target_pairs={{128,0},{144,16},{160,32},{176,48},{192,64},{208,80},{224,96},{240... | collective-permute-start | bytes 589832 | tf_op jit(solution)/shard_map/ppermute | solution.py:32
  122.9 1.1 collective-permute-start.40
  124.0 2.7 %collective-permute-start.36 = (bf16[512,128]{1,0:T(8,128)(2,1)S(1)}, bf16[512,128]{1,0:T(8,128)(2,1)S(1)}, u32[]{:S(2)}, u32[]{:S(2)}) collective-permute-start(bf16[512,128]{1,0:T(8,128)(2,1)S(1)} %get-tuple-element.133), channel_id=1, source_target_pairs={{32,0},{48,16},{0,32},{16,48},{96,64},{112,80},{64,96},{80,112},{1... | collective-permute-start | bytes 393224 | tf_op jit(solution)/shard_map/ppermute | solution.py:32
  126.7 0.6 collective-permute-start.37
  127.3 5.4 %collective-permute-done.36 = bf16[512,128]{1,0:T(8,128)(2,1)S(1)} collective-permute-done((bf16[512,128]{1,0:T(8,128)(2,1)S(1)}, bf16[512,128]{1,0:T(8,128)(2,1)S(1)}, u32[]{:S(2)}, u32[]{:S(2)}) %collective-permute-start.36) | collective-permute-done | bytes 131104 | tf_op jit(solution)/shard_map/ppermute | solution.py:32
  132.8 2.9 %collective-permute-start.43 = (bf16[256,128]{1,0:T(8,128)(2,1)S(1)}, bf16[256,128]{1,0:T(8,128)(2,1)S(1)}, u32[]{:S(2)}, u32[]{:S(2)}) collective-permute-start(bf16[256,128]{1,0:T(8,128)(2,1)S(1)} %add_convert_fusion.10), channel_id=1, source_target_pairs={{12,0},{13,1},{14,2},{15,3},{0,4},{1,5},{2,6},{3,7},{4,8},{5,9},{6... | collective-permute-start | bytes 196616 | tf_op jit(solution)/shard_map/ppermute | solution.py:46
  135.6 0.6 collective-permute-start.42
  136.2 0.7 collective-permute-start.41
  137.0 0.8 collective-permute-done.43
  137.8 3.7 %collective-permute-done.42 = bf16[256,128]{1,0:T(8,128)(2,1)S(1)} collective-permute-done((bf16[256,128]{1,0:T(8,128)(2,1)S(1)}, bf16[256,128]{1,0:T(8,128)(2,1)S(1)}, u32[]{:S(2)}, u32[]{:S(2)}) %collective-permute-start.42) | collective-permute-done | bytes 65568 | tf_op jit(solution)/shard_map/ppermute | solution.py:46
  141.5 0.7 collective-permute-done.41
  142.2 1.0 fusion
  143.8 0.6 shard_map.95
  144.4 1.1 convert_multiply_fusion
  (82 shorter events, 6.1 us)
Async XLA Ops:
  0.6 25.7 %collective-permute-start.10 = (bf16[128,512]{1,0:T(8,128)(2,1)}, bf16[128,512]{1,0:T(8,128)(2,1)S(1)}, u32[]{:S(2)}, u32[]{:S(2)}) collective-permute-start(bf16[128,512]{1,0:T(8,128)(2,1)} %bitcast.26), channel_id=1, source_target_pairs={{192,0},{208,16},{224,32},{240,48},{0,64},{16,80},{32,96},{48,112}... | collective-permute-start | bytes 393224 | tf_op jit(solution)/shard_map/ppermute | solution.py:32
  2.3 17.6 %collective-permute-start.3 = (bf16[128,512]{1,0:T(8,128)(2,1)}, bf16[128,512]{1,0:T(8,128)(2,1)S(1)}, u32[]{:S(2)}, u32[]{:S(2)}) collective-permute-start(bf16[128,512]{1,0:T(8,128)(2,1)} %bitcast.27), channel_id=1, source_target_pairs={{128,0},{144,16},{160,32},{176,48},{192,64},{208,80},{224,96},{240... | collective-permute-start | bytes 393224 | tf_op jit(solution)/shard_map/ppermute | solution.py:32
  5.2 15.6 %collective-permute-start.2 = (bf16[128,512]{1,0:T(8,128)(2,1)}, bf16[128,512]{1,0:T(8,128)(2,1)S(1)}, u32[]{:S(2)}, u32[]{:S(2)}) collective-permute-start(bf16[128,512]{1,0:T(8,128)(2,1)} %bitcast.28), channel_id=1, source_target_pairs={{48,0},{0,16},{16,32},{32,48},{112,64},{64,80},{80,96},{96,112},{1... | collective-permute-start | bytes 393224 | tf_op jit(solution)/shard_map/ppermute | solution.py:32
  7.1 13.7 %collective-permute-start.1 = (bf16[128,512]{1,0:T(8,128)(2,1)}, bf16[128,512]{1,0:T(8,128)(2,1)S(1)}, u32[]{:S(2)}, u32[]{:S(2)}) collective-permute-start(bf16[128,512]{1,0:T(8,128)(2,1)} %bitcast.29), channel_id=1, source_target_pairs={{32,0},{48,16},{0,32},{16,48},{96,64},{112,80},{64,96},{80,112},{1... | collective-permute-start | bytes 393224 | tf_op jit(solution)/shard_map/ppermute | solution.py:32
  10.4 10.4 %collective-permute-start = (bf16[128,512]{1,0:T(8,128)(2,1)}, bf16[128,512]{1,0:T(8,128)(2,1)S(1)}, u32[]{:S(2)}, u32[]{:S(2)}) collective-permute-start(bf16[128,512]{1,0:T(8,128)(2,1)} %bitcast.30), channel_id=1, source_target_pairs={{16,0},{32,16},{48,32},{0,48},{80,64},{96,80},{112,96},{64,112},{1... | collective-permute-start | bytes 393224 | tf_op jit(solution)/shard_map/ppermute | solution.py:32
  13.4 2.2 %copy-start = (bf16[1,1,128,128,128]{4,3,2,1,0:T(8,128)(2,1)S(1)}, bf16[1,1,128,128,128]{4,3,2,1,0:T(8,128)(2,1)}, u32[]{:S(2)}) copy-start(bf16[1,1,128,128,128]{4,3,2,1,0:T(8,128)(2,1)} %param.9) | copy-start | bytes 12582916
  15.6 4.2 %copy-start.3 = (bf16[1,128,512]{2,1,0:T(8,128)(2,1)S(1)}, bf16[1,128,512]{2,1,0:T(8,128)(2,1)}, u32[]{:S(2)}) copy-start(bf16[1,128,512]{2,1,0:T(8,128)(2,1)} %param.6) | copy-start | bytes 393220
  19.8 5.9 %collective-permute-start.9 = (bf16[128,512]{1,0:T(8,128)(2,1)S(1)}, bf16[128,512]{1,0:T(8,128)(2,1)S(1)}, u32[]{:S(2)}, u32[]{:S(2)}) collective-permute-start(bf16[128,512]{1,0:T(8,128)(2,1)S(1)} %bitcast.31), channel_id=1, source_target_pairs={{64,0},{80,16},{96,32},{112,48},{128,64},{144,80},{160,96},{176,11... | collective-permute-start | bytes 393224 | tf_op jit(solution)/shard_map/ppermute | solution.py:32
  20.8 13.8 %collective-permute-start.8 = (bf16[128,512]{1,0:T(8,128)(2,1)S(1)}, bf16[128,512]{1,0:T(8,128)(2,1)S(1)}, u32[]{:S(2)}, u32[]{:S(2)}) collective-permute-start(bf16[128,512]{1,0:T(8,128)(2,1)S(1)} %collective-permute-done.1), channel_id=1, source_target_pairs={{128,0},{144,16},{160,32},{176,48},{192,64},{208,80},{224,96},{240... | collective-permute-start | bytes 393224 | tf_op jit(solution)/shard_map/ppermute | solution.py:32
  21.0 14.6 %collective-permute-start.5 = (bf16[384,512]{1,0:T(8,128)(2,1)S(1)}, bf16[384,512]{1,0:T(8,128)(2,1)S(1)}, u32[]{:S(2)}, u32[]{:S(2)}) collective-permute-start(bf16[384,512]{1,0:T(8,128)(2,1)S(1)} %get-tuple-element.155), channel_id=1, source_target_pairs={{192,0},{208,16},{224,32},{240,48},{0,64},{16,80},{32,96},{48,112}... | collective-permute-start | bytes 1179656 | tf_op jit(solution)/shard_map/ppermute | solution.py:32
  22.2 13.4 %collective-permute-start.4 = (bf16[384,512]{1,0:T(8,128)(2,1)S(1)}, bf16[384,512]{1,0:T(8,128)(2,1)S(1)}, u32[]{:S(2)}, u32[]{:S(2)}) collective-permute-start(bf16[384,512]{1,0:T(8,128)(2,1)S(1)} %get-tuple-element.155), channel_id=1, source_target_pairs={{64,0},{80,16},{96,32},{112,48},{128,64},{144,80},{160,96},{176,11... | collective-permute-start | bytes 1179656 | tf_op jit(solution)/shard_map/ppermute | solution.py:32
  25.8 8.9 %collective-permute-start.7 = (bf16[128,512]{1,0:T(8,128)(2,1)S(1)}, bf16[128,512]{1,0:T(8,128)(2,1)S(1)}, u32[]{:S(2)}, u32[]{:S(2)}) collective-permute-start(bf16[128,512]{1,0:T(8,128)(2,1)S(1)} %collective-permute-done.3), channel_id=1, source_target_pairs={{48,0},{0,16},{16,32},{32,48},{112,64},{64,80},{80,96},{96,112},{1... | collective-permute-start | bytes 393224 | tf_op jit(solution)/shard_map/ppermute | solution.py:32
  26.3 8.3 %collective-permute-start.6 = (bf16[128,512]{1,0:T(8,128)(2,1)S(1)}, bf16[128,512]{1,0:T(8,128)(2,1)S(1)}, u32[]{:S(2)}, u32[]{:S(2)}) collective-permute-start(bf16[128,512]{1,0:T(8,128)(2,1)S(1)} %collective-permute-done.3), channel_id=1, source_target_pairs={{16,0},{32,16},{48,32},{0,48},{80,64},{96,80},{112,96},{64,112},{1... | collective-permute-start | bytes 393224 | tf_op jit(solution)/shard_map/ppermute | solution.py:32
  36.6 2.9 %collective-permute-start.11 = (bf16[512,512]{1,0:T(8,128)(2,1)S(1)}, bf16[512,512]{1,0:T(8,128)(2,1)S(1)}, u32[]{:S(2)}, u32[]{:S(2)}) collective-permute-start(bf16[512,512]{1,0:T(8,128)(2,1)S(1)} %shard_map.87), channel_id=1, source_target_pairs={{1,0},{0,1},{3,2},{2,3},{5,4},{4,5},{7,6},{6,7},{9,8},{8,9},{11,10... | collective-permute-start | bytes 1572872 | tf_op jit(solution)/shard_map/ppermute | solution.py:46
  39.5 16.6 %collective-permute-start.12 = (bf16[512,512]{1,0:T(8,128)(2,1)S(1)}, bf16[512,512]{1,0:T(8,128)(2,1)S(1)}, u32[]{:S(2)}, u32[]{:S(2)}) collective-permute-start(bf16[512,512]{1,0:T(8,128)(2,1)S(1)} %slice.152), channel_id=1, source_target_pairs={{1,0},{0,1},{3,2},{2,3},{5,4},{4,5},{7,6},{6,7},{9,8},{8,9},{11,10... | collective-permute-start | bytes 1572872 | tf_op jit(solution)/shard_map/ppermute | solution.py:46
  40.2 5.5 %collective-permute-start.13 = (bf16[128,512]{1,0:T(8,128)(2,1)S(1)}, bf16[128,512]{1,0:T(8,128)(2,1)S(1)}, u32[]{:S(2)}, u32[]{:S(2)}) collective-permute-start(bf16[128,512]{1,0:T(8,128)(2,1)S(1)} %get-tuple-element.151), channel_id=1, source_target_pairs={{12,0},{13,1},{14,2},{15,3},{0,4},{1,5},{2,6},{3,7},{4,8},{5,9},{6... | collective-permute-start | bytes 393224 | tf_op jit(solution)/shard_map/ppermute | solution.py:46
  41.9 9.2 %collective-permute-start.15 = (bf16[128,512]{1,0:T(8,128)(2,1)S(1)}, bf16[128,512]{1,0:T(8,128)(2,1)S(1)}, u32[]{:S(2)}, u32[]{:S(2)}) collective-permute-start(bf16[128,512]{1,0:T(8,128)(2,1)S(1)} %get-tuple-element.152), channel_id=1, source_target_pairs={{4,0},{5,1},{6,2},{7,3},{8,4},{9,5},{10,6},{11,7},{12,8},{13,9},{1... | collective-permute-start | bytes 393224 | tf_op jit(solution)/shard_map/ppermute | solution.py:46
  42.3 8.8 %collective-permute-start.14 = (bf16[128,512]{1,0:T(8,128)(2,1)S(1)}, bf16[128,512]{1,0:T(8,128)(2,1)S(1)}, u32[]{:S(2)}, u32[]{:S(2)}) collective-permute-start(bf16[128,512]{1,0:T(8,128)(2,1)S(1)} %get-tuple-element.153), channel_id=1, source_target_pairs={{8,0},{9,1},{10,2},{11,3},{12,4},{13,5},{14,6},{15,7},{0,8},{1,9},... | collective-permute-start | bytes 393224 | tf_op jit(solution)/shard_map/ppermute | solution.py:46
  51.2 14.1 %copy-start.1 = (bf16[512,512]{1,0:T(8,128)(2,1)S(1)}, bf16[512,512]{1,0:T(8,128)(2,1)}, u32[]{:S(2)}) copy-start(bf16[512,512]{1,0:T(8,128)(2,1)} %weight_ref.1) | copy-start | bytes 1572868
  51.2 14.1 %copy-start.2 = (bf16[1,128,512]{2,1,0:T(8,128)(2,1)S(1)}, bf16[1,128,512]{2,1,0:T(8,128)(2,1)}, u32[]{:S(2)}) copy-start(bf16[1,128,512]{2,1,0:T(8,128)(2,1)} %param.11) | copy-start | bytes 393220
  51.2 10.4 %collective-permute-start.16 = (bf16[128,512]{1,0:T(8,128)(2,1)S(1)}, bf16[128,512]{1,0:T(8,128)(2,1)S(1)}, u32[]{:S(2)}, u32[]{:S(2)}) collective-permute-start(bf16[128,512]{1,0:T(8,128)(2,1)S(1)} %add_convert_fusion.4), channel_id=1, source_target_pairs={{2,0},{3,1},{0,2},{1,3},{6,4},{7,5},{4,6},{5,7},{10,8},{11,9},{8,1... | collective-permute-start | bytes 393224 | tf_op jit(solution)/shard_map/ppermute | solution.py:46
  56.3 8.4 %collective-permute-start.19 = (bf16[128,512]{1,0:T(8,128)(2,1)S(1)}, bf16[128,512]{1,0:T(8,128)(2,1)S(1)}, u32[]{:S(2)}, u32[]{:S(2)}) collective-permute-start(bf16[128,512]{1,0:T(8,128)(2,1)S(1)} %get-tuple-element.147), channel_id=1, source_target_pairs={{4,0},{5,1},{6,2},{7,3},{8,4},{9,5},{10,6},{11,7},{12,8},{13,9},{1... | collective-permute-start | bytes 393224 | tf_op jit(solution)/shard_map/ppermute | solution.py:46
  56.4 8.3 %collective-permute-start.18 = (bf16[128,512]{1,0:T(8,128)(2,1)S(1)}, bf16[128,512]{1,0:T(8,128)(2,1)S(1)}, u32[]{:S(2)}, u32[]{:S(2)}) collective-permute-start(bf16[128,512]{1,0:T(8,128)(2,1)S(1)} %get-tuple-element.148), channel_id=1, source_target_pairs={{8,0},{9,1},{10,2},{11,3},{12,4},{13,5},{14,6},{15,7},{0,8},{1,9},... | collective-permute-start | bytes 393224 | tf_op jit(solution)/shard_map/ppermute | solution.py:46
  59.2 6.1 %collective-permute-start.17 = (bf16[128,512]{1,0:T(8,128)(2,1)S(1)}, bf16[128,512]{1,0:T(8,128)(2,1)S(1)}, u32[]{:S(2)}, u32[]{:S(2)}) collective-permute-start(bf16[128,512]{1,0:T(8,128)(2,1)S(1)} %get-tuple-element.149), channel_id=1, source_target_pairs={{12,0},{13,1},{14,2},{15,3},{0,4},{1,5},{2,6},{3,7},{4,8},{5,9},{6... | collective-permute-start | bytes 393224 | tf_op jit(solution)/shard_map/ppermute | solution.py:46
  66.8 11.9 %collective-permute-start.20 = (bf16[1024,128]{1,0:T(8,128)(2,1)S(1)}, bf16[1024,128]{1,0:T(8,128)(2,1)S(1)}, u32[]{:S(2)}, u32[]{:S(2)}) collective-permute-start(bf16[1024,128]{1,0:T(8,128)(2,1)S(1)} %get-tuple-element.95), channel_id=1, source_target_pairs={{2,0},{3,1},{0,2},{1,3},{6,4},{7,5},{4,6},{5,7},{10,8},{11,9},{8,1... | collective-permute-start | bytes 786440 | tf_op jit(solution)/shard_map/ppermute | solution.py:46
  68.0 7.1 %collective-permute-start.21 = (bf16[640,128]{1,0:T(8,128)(2,1)S(1)}, bf16[640,128]{1,0:T(8,128)(2,1)S(1)}, u32[]{:S(2)}, u32[]{:S(2)}) collective-permute-start(bf16[640,128]{1,0:T(8,128)(2,1)S(1)} %get-tuple-element.96), channel_id=1, source_target_pairs={{4,0},{5,1},{6,2},{7,3},{8,4},{9,5},{10,6},{11,7},{12,8},{13,9},{1... | collective-permute-start | bytes 491528 | tf_op jit(solution)/shard_map/ppermute | solution.py:46
  68.3 8.6 %collective-permute-start.22 = (bf16[640,128]{1,0:T(8,128)(2,1)S(1)}, bf16[640,128]{1,0:T(8,128)(2,1)S(1)}, u32[]{:S(2)}, u32[]{:S(2)}) collective-permute-start(bf16[640,128]{1,0:T(8,128)(2,1)S(1)} %get-tuple-element.97), channel_id=1, source_target_pairs={{8,0},{9,1},{10,2},{11,3},{12,4},{13,5},{14,6},{15,7},{0,8},{1,9},... | collective-permute-start | bytes 491528 | tf_op jit(solution)/shard_map/ppermute | solution.py:46
  71.8 5.4 %collective-permute-start.23 = (bf16[640,128]{1,0:T(8,128)(2,1)S(1)}, bf16[640,128]{1,0:T(8,128)(2,1)S(1)}, u32[]{:S(2)}, u32[]{:S(2)}) collective-permute-start(bf16[640,128]{1,0:T(8,128)(2,1)S(1)} %get-tuple-element.98), channel_id=1, source_target_pairs={{12,0},{13,1},{14,2},{15,3},{0,4},{1,5},{2,6},{3,7},{4,8},{5,9},{6... | collective-permute-start | bytes 491528 | tf_op jit(solution)/shard_map/ppermute | solution.py:46
  78.8 6.1 %collective-permute-start.27 = (bf16[640,512]{1,0:T(8,128)(2,1)S(1)}, bf16[640,512]{1,0:T(8,128)(2,1)S(1)}, u32[]{:S(2)}, u32[]{:S(2)}) collective-permute-start(bf16[640,512]{1,0:T(8,128)(2,1)S(1)} %pad_maximum_fusion), channel_id=1, source_target_pairs={{1,0},{0,1},{3,2},{2,3},{5,4},{4,5},{7,6},{6,7},{9,8},{8,9},{11,10... | collective-permute-start | bytes 1966088 | tf_op jit(solution)/shard_map/ppermute | solution.py:46
  79.6 9.3 %collective-permute-start.24 = (bf16[640,128]{1,0:T(8,128)(2,1)S(1)}, bf16[640,128]{1,0:T(8,128)(2,1)S(1)}, u32[]{:S(2)}, u32[]{:S(2)}) collective-permute-start(bf16[640,128]{1,0:T(8,128)(2,1)S(1)} %get-tuple-element.101), channel_id=1, source_target_pairs={{4,0},{5,1},{6,2},{7,3},{8,4},{9,5},{10,6},{11,7},{12,8},{13,9},{1... | collective-permute-start | bytes 491528 | tf_op jit(solution)/shard_map/ppermute | solution.py:46
  81.1 11.7 %collective-permute-start.25 = (bf16[640,128]{1,0:T(8,128)(2,1)S(1)}, bf16[640,128]{1,0:T(8,128)(2,1)S(1)}, u32[]{:S(2)}, u32[]{:S(2)}) collective-permute-start(bf16[640,128]{1,0:T(8,128)(2,1)S(1)} %get-tuple-element.102), channel_id=1, source_target_pairs={{8,0},{9,1},{10,2},{11,3},{12,4},{13,5},{14,6},{15,7},{0,8},{1,9},... | collective-permute-start | bytes 491528 | tf_op jit(solution)/shard_map/ppermute | solution.py:46
  84.7 8.1 %collective-permute-start.26 = (bf16[640,128]{1,0:T(8,128)(2,1)S(1)}, bf16[640,128]{1,0:T(8,128)(2,1)S(1)}, u32[]{:S(2)}, u32[]{:S(2)}) collective-permute-start(bf16[640,128]{1,0:T(8,128)(2,1)S(1)} %get-tuple-element.103), channel_id=1, source_target_pairs={{12,0},{13,1},{14,2},{15,3},{0,4},{1,5},{2,6},{3,7},{4,8},{5,9},{6... | collective-permute-start | bytes 491528 | tf_op jit(solution)/shard_map/ppermute | solution.py:46
  92.8 2.2 %collective-permute-start.28 = (bf16[640,512]{1,0:T(8,128)(2,1)S(1)}, bf16[640,512]{1,0:T(8,128)(2,1)S(1)}, u32[]{:S(2)}, u32[]{:S(2)}) collective-permute-start(bf16[640,512]{1,0:T(8,128)(2,1)S(1)} %pad_maximum_fusion.1), channel_id=1, source_target_pairs={{1,0},{0,1},{3,2},{2,3},{5,4},{4,5},{7,6},{6,7},{9,8},{8,9},{11,10... | collective-permute-start | bytes 1966088 | tf_op jit(solution)/shard_map/ppermute | solution.py:46
  99.3 18.9 %collective-permute-start.31 = (bf16[512,384]{1,0:T(8,128)(2,1)S(1)}, bf16[512,384]{1,0:T(8,128)(2,1)S(1)}, u32[]{:S(2)}, u32[]{:S(2)}) collective-permute-start(bf16[512,384]{1,0:T(8,128)(2,1)S(1)} %get-tuple-element.123), channel_id=1, source_target_pairs={{192,0},{208,16},{224,32},{240,48},{0,64},{16,80},{32,96},{48,112}... | collective-permute-start | bytes 1179656 | tf_op jit(solution)/shard_map/ppermute | solution.py:32
  100.5 17.7 %collective-permute-start.32 = (bf16[512,384]{1,0:T(8,128)(2,1)S(1)}, bf16[512,384]{1,0:T(8,128)(2,1)S(1)}, u32[]{:S(2)}, u32[]{:S(2)}) collective-permute-start(bf16[512,384]{1,0:T(8,128)(2,1)S(1)} %get-tuple-element.124), channel_id=1, source_target_pairs={{64,0},{80,16},{96,32},{112,48},{128,64},{144,80},{160,96},{176,11... | collective-permute-start | bytes 1179656 | tf_op jit(solution)/shard_map/ppermute | solution.py:32
  103.4 5.2 %collective-permute-start.30 = (bf16[256,128]{1,0:T(8,128)(2,1)S(1)}, bf16[256,128]{1,0:T(8,128)(2,1)S(1)}, u32[]{:S(2)}, u32[]{:S(2)}) collective-permute-start(bf16[256,128]{1,0:T(8,128)(2,1)S(1)} %get-tuple-element.117.w0_ref), channel_id=1, source_target_pairs={{32,0},{48,16},{0,32},{16,48},{96,64},{112,80},{64,96},{80,112},{1... | collective-permute-start | bytes 196616 | tf_op jit(solution)/shard_map/ppermute | solution.py:32
  105.2 11.5 %collective-permute-start.29 = (bf16[512,128]{1,0:T(8,128)(2,1)S(1)}, bf16[512,128]{1,0:T(8,128)(2,1)S(1)}, u32[]{:S(2)}, u32[]{:S(2)}) collective-permute-start(bf16[512,128]{1,0:T(8,128)(2,1)S(1)} %get-tuple-element.116), channel_id=1, source_target_pairs={{128,0},{144,16},{160,32},{176,48},{192,64},{208,80},{224,96},{240... | collective-permute-start | bytes 393224 | tf_op jit(solution)/shard_map/ppermute | solution.py:32
  105.4 12.8 %collective-permute-start.33 = (bf16[768,128]{1,0:T(8,128)(2,1)S(1)}, bf16[768,128]{1,0:T(8,128)(2,1)S(1)}, u32[]{:S(2)}, u32[]{:S(2)}) collective-permute-start(bf16[768,128]{1,0:T(8,128)(2,1)S(1)} %get-tuple-element.125), channel_id=1, source_target_pairs={{48,0},{0,16},{16,32},{32,48},{112,64},{64,80},{80,96},{96,112},{1... | collective-permute-start | bytes 589832 | tf_op jit(solution)/shard_map/ppermute | solution.py:32
  108.6 9.6 %collective-permute-start.34 = (bf16[768,128]{1,0:T(8,128)(2,1)S(1)}, bf16[768,128]{1,0:T(8,128)(2,1)S(1)}, u32[]{:S(2)}, u32[]{:S(2)}) collective-permute-start(bf16[768,128]{1,0:T(8,128)(2,1)S(1)} %get-tuple-element.126), channel_id=1, source_target_pairs={{16,0},{32,16},{48,32},{0,48},{80,64},{96,80},{112,96},{64,112},{1... | collective-permute-start | bytes 589832 | tf_op jit(solution)/shard_map/ppermute | solution.py:32
  118.4 8.3 %collective-permute-start.35 = (bf16[512,128]{1,0:T(8,128)(2,1)S(1)}, bf16[512,128]{1,0:T(8,128)(2,1)S(1)}, u32[]{:S(2)}, u32[]{:S(2)}) collective-permute-start(bf16[512,128]{1,0:T(8,128)(2,1)S(1)} %get-tuple-element.132), channel_id=1, source_target_pairs={{48,0},{0,16},{16,32},{32,48},{112,64},{64,80},{80,96},{96,112},{1... | collective-permute-start | bytes 393224 | tf_op jit(solution)/shard_map/ppermute | solution.py:32
  119.2 13.5 %collective-permute-start.38 = (bf16[768,128]{1,0:T(8,128)(2,1)S(1)}, bf16[768,128]{1,0:T(8,128)(2,1)S(1)}, u32[]{:S(2)}, u32[]{:S(2)}) collective-permute-start(bf16[768,128]{1,0:T(8,128)(2,1)S(1)} %get-tuple-element.135), channel_id=1, source_target_pairs={{192,0},{208,16},{224,32},{240,48},{0,64},{16,80},{32,96},{48,112}... | collective-permute-start | bytes 589832 | tf_op jit(solution)/shard_map/ppermute | solution.py:32
  120.6 12.2 %collective-permute-start.39 = (bf16[768,128]{1,0:T(8,128)(2,1)S(1)}, bf16[768,128]{1,0:T(8,128)(2,1)S(1)}, u32[]{:S(2)}, u32[]{:S(2)}) collective-permute-start(bf16[768,128]{1,0:T(8,128)(2,1)S(1)} %get-tuple-element.136), channel_id=1, source_target_pairs={{128,0},{144,16},{160,32},{176,48},{192,64},{208,80},{224,96},{240... | collective-permute-start | bytes 589832 | tf_op jit(solution)/shard_map/ppermute | solution.py:32
  122.9 9.8 %collective-permute-start.40 = (bf16[768,128]{1,0:T(8,128)(2,1)S(1)}, bf16[768,128]{1,0:T(8,128)(2,1)S(1)}, u32[]{:S(2)}, u32[]{:S(2)}) collective-permute-start(bf16[768,128]{1,0:T(8,128)(2,1)S(1)} %get-tuple-element.137), channel_id=1, source_target_pairs={{64,0},{80,16},{96,32},{112,48},{128,64},{144,80},{160,96},{176,11... | collective-permute-start | bytes 589832 | tf_op jit(solution)/shard_map/ppermute | solution.py:32
  124.0 8.7 %collective-permute-start.36 = (bf16[512,128]{1,0:T(8,128)(2,1)S(1)}, bf16[512,128]{1,0:T(8,128)(2,1)S(1)}, u32[]{:S(2)}, u32[]{:S(2)}) collective-permute-start(bf16[512,128]{1,0:T(8,128)(2,1)S(1)} %get-tuple-element.133), channel_id=1, source_target_pairs={{32,0},{48,16},{0,32},{16,48},{96,64},{112,80},{64,96},{80,112},{1... | collective-permute-start | bytes 393224 | tf_op jit(solution)/shard_map/ppermute | solution.py:32
  126.7 6.0 %collective-permute-start.37 = (bf16[512,128]{1,0:T(8,128)(2,1)S(1)}, bf16[512,128]{1,0:T(8,128)(2,1)S(1)}, u32[]{:S(2)}, u32[]{:S(2)}) collective-permute-start(bf16[512,128]{1,0:T(8,128)(2,1)S(1)} %get-tuple-element.134), channel_id=1, source_target_pairs={{16,0},{32,16},{48,32},{0,48},{80,64},{96,80},{112,96},{64,112},{1... | collective-permute-start | bytes 393224 | tf_op jit(solution)/shard_map/ppermute | solution.py:32
  132.8 5.0 %collective-permute-start.43 = (bf16[256,128]{1,0:T(8,128)(2,1)S(1)}, bf16[256,128]{1,0:T(8,128)(2,1)S(1)}, u32[]{:S(2)}, u32[]{:S(2)}) collective-permute-start(bf16[256,128]{1,0:T(8,128)(2,1)S(1)} %add_convert_fusion.10), channel_id=1, source_target_pairs={{12,0},{13,1},{14,2},{15,3},{0,4},{1,5},{2,6},{3,7},{4,8},{5,9},{6... | collective-permute-start | bytes 196616 | tf_op jit(solution)/shard_map/ppermute | solution.py:46
  135.6 5.8 %collective-permute-start.42 = (bf16[256,128]{1,0:T(8,128)(2,1)S(1)}, bf16[256,128]{1,0:T(8,128)(2,1)S(1)}, u32[]{:S(2)}, u32[]{:S(2)}) collective-permute-start(bf16[256,128]{1,0:T(8,128)(2,1)S(1)} %add_convert_fusion.10), channel_id=1, source_target_pairs={{8,0},{9,1},{10,2},{11,3},{12,4},{13,5},{14,6},{15,7},{0,8},{1,9},... | collective-permute-start | bytes 196616 | tf_op jit(solution)/shard_map/ppermute | solution.py:46
  136.2 5.9 %collective-permute-start.41 = (bf16[256,128]{1,0:T(8,128)(2,1)S(1)}, bf16[256,128]{1,0:T(8,128)(2,1)S(1)}, u32[]{:S(2)}, u32[]{:S(2)}) collective-permute-start(bf16[256,128]{1,0:T(8,128)(2,1)S(1)} %add_convert_fusion.10), channel_id=1, source_target_pairs={{4,0},{5,1},{6,2},{7,3},{8,4},{9,5},{10,6},{11,7},{12,8},{13,9},{1... | collective-permute-start | bytes 196616 | tf_op jit(solution)/shard_map/ppermute | solution.py:46
  142.1 1.6 %collective-permute-start.44 = (bf16[1024,128]{1,0:T(8,128)(2,1)S(1)}, bf16[1024,128]{1,0:T(8,128)(2,1)S(1)}, u32[]{:S(2)}, u32[]{:S(2)}) collective-permute-start(bf16[1024,128]{1,0:T(8,128)(2,1)S(1)} %pad_maximum_fusion.2.own_ref), channel_id=1, source_target_pairs={{1,0},{0,1},{3,2},{2,3},{5,4},{4,5},{7,6},{6,7},{9,8},{8,9},{11,10... | collective-permute-start | bytes 786440 | tf_op jit(solution)/shard_map/ppermute | solution.py:46
where the time goes:
time: 147 us; the launch traced here: 146 us
  starting transfers between devices  70.8 us (48%)
  waiting for transfers between devices  40.7 us (28%)
  Pallas kernels  24.9 us (17%)
  local copies, waits for them, and re-layouts  3.17 us (2%)
  other arithmetic  3.15 us (2%)
  between operations  1.79 us (1%)
    ppermute x23, starting transfers between devices, row_shift(): return lax.ppermute(data, 'row', pairs)  41.7 us
    ppermute x22, waiting for transfers between devices, col_shift(): return lax.ppermute(data, 'col', pairs)  29.2 us
    ppermute x22, starting transfers between devices, col_shift(): return lax.ppermute(data, 'col', pairs)  29 us
    pallas_call x7, Pallas kernels, call(): pl.pallas_call(kernel, out_shape=shapes, in_specs=[pl.BlockSpec(memory_sp...  12.5 us
    ppermute x23, waiting for transfers between devices, row_shift(): return lax.ppermute(data, 'row', pairs)  11.5 us
    pallas_call x3, Pallas kernels, products(): pl.pallas_call(functools.partial(products_kernel, size, pieces, added is...  8.28 us
    pallas_call x1, Pallas kernels, densify(): pl.pallas_call(functools.partial(densify_kernel, [first for first, _ in p...  4.18 us
  transfers between devices with their start and end apart: 45, of which 20 were waited for; matrix products, arithmetic and copies ran while one was open for 3% of the time, Pallas kernels for 12%

commit v1 on v0

--- a/solution.py
+++ b/solution.py
@@ -247,8 +247,25 @@
     split_for_x(me_ref[0], both_ref, outs)
 
 
-def first_kernel(dense1_ref, dense2_ref, source_ref, near_ref, far_ref):
+def weight_rows(source_ref, total_ref):
+    full = total_ref.shape[1]
+
+    def step(i, _):
+        here = pl.ds(pl.multiple_of(i * STEP, STEP), STEP)
+        total_ref[:, here] = lax.dot_general(
+            source_ref[full:, :],
+            source_ref[here, :],
+            (((1,), (1,)), ((), ())),
+            preferred_element_type=jnp.float32,
+        )
+        return 0
+
+    lax.fori_loop(0, full // STEP, step, 0)
+
+
+def first_kernel(dense1_ref, dense2_ref, source_ref, near_ref, far_ref, total_ref):
     nodes = source_ref.shape[1]
+    weight_rows(source_ref, total_ref)
     for dense_ref, ref in ((dense1_ref, near_ref), (dense2_ref, far_ref)):
 
         def step(i, _):
@@ -260,24 +277,12 @@
 
 
 def lead_kernel(me_ref, dense_ref, source_ref, first_ref, added_ref, *refs):
-    lead1, over1, lead2, over3, lead3, w_ref, *totals = refs
+    lead1, over1, lead2, over3, lead3, w_ref, total_ref = refs
     full, nodes = lead1.shape[0], source_ref.shape[1]
-    for ref, total_ref in zip((first_ref, source_ref), totals):
-
-        def step(i, _):
-            here = pl.ds(pl.multiple_of(i * TILE, TILE), TILE)
-            total_ref[:, here] = lax.dot_general(
-                ref[full:, :],
-                ref[here, :],
-                (((1,), (1,)), ((), ())),
-                preferred_element_type=jnp.float32,
-            )
-            return 0
-
-        lax.fori_loop(0, full // TILE, step, 0)
+    weight_rows(source_ref, total_ref)
     rows = w_ref.shape[0] * TILE // full
     span = pl.ds(pl.multiple_of(me_ref[1] * rows, rows), rows)
-    w = bf16(totals[0][span, :] + totals[1][span, :])
+    w = bf16(first_ref[span, :] + total_ref[span, :])
     for i in range(full // TILE):
         w_ref[i * rows : (i + 1) * rows, :] = w[:, i * TILE : (i + 1) * TILE]
 
@@ -411,14 +416,14 @@
     own_core = col_shift(own, "k", 1)
     other_parts = [col_shift(other_sent[s], "x", s) for s in (1, 2, 3)]
     first = jnp.concatenate([own, own_core], axis=1)
-    near, far = call(
+    near, far, w_first = call(
         first_kernel,
-        [((full, 7 * TILE), F32), ((full, 9 * TILE), F32)],
+        [((full, 7 * TILE), F32), ((full, 9 * TILE), F32), ((TILE, full), F32)],
         *forward,
         first,
         flops=2 * 16 * TILE * full * 8 * TILE,
     )
-    other_parts, near, far, first = join(other_parts, near, far, first)
+    other_parts, near, far, w_first = join(other_parts, near, far, w_first)
     other = jnp.concatenate([other_sent[0]] + other_parts, axis=1)
     source = jnp.concatenate([other, col_shift(other, "k", 1)], axis=1)
 
@@ -430,9 +435,9 @@
         me,
         forward[1],
         source,
-        first,
+        w_first,
         far,
-        scratch=[pltpu.VMEM((TILE, full), F32)] * 2,
+        scratch=[pltpu.VMEM((TILE, full), F32)],
         scalars=1,
         flops=2 * 9 * TILE * full * 8 * TILE,
     )

time: 147 us -> 147 us (level)
  waiting for transfers between devices: 40.7 us -> 47.8 us
  starting transfers between devices: 70.8 us -> 64.6 us
  Pallas kernels: 24.9 us -> 22.9 us
    ppermute x23, waiting for transfers between devices: 11.5 us -> 17 us  [row_shift(): return lax.ppermute(data, 'row', pairs)]
    ppermute x23, starting transfers between devices: 41.7 us -> 38.6 us  [row_shift(): return lax.ppermute(data, 'row', pairs)]
    ppermute x22, starting transfers between devices: 29 us -> 26 us  [col_shift(): return lax.ppermute(data, 'col', pairs)]
    ppermute x22, waiting for transfers between devices: 29.2 us -> 30.8 us  [col_shift(): return lax.ppermute(data, 'col', pairs)]
  transfers between devices with their start and end apart: 45 -> 45, of which waited for: 20 -> 23; matrix products, arithmetic and copies ran while one was open for 3% -> 3% of each run, Pallas kernels for 12% -> 12%
where the time goes in v1:
time: 147 us; the launch traced here: 144 us
  starting transfers between devices  64.6 us (44%)
  waiting for transfers between devices  47.8 us (33%)
  Pallas kernels  22.9 us (16%)
  local copies, waits for them, and re-layouts  3.16 us (2%)
  other arithmetic  3.15 us (2%)
  between operations  1.77 us (1%)
    ppermute x23, starting transfers between devices, row_shift(): return lax.ppermute(data, 'row', pairs)  38.6 us
    ppermute x22, waiting for transfers between devices, col_shift(): return lax.ppermute(data, 'col', pairs)  30.8 us
    ppermute x22, starting transfers between devices, col_shift(): return lax.ppermute(data, 'col', pairs)  26 us
    ppermute x23, waiting for transfers between devices, row_shift(): return lax.ppermute(data, 'row', pairs)  17 us
    pallas_call x7, Pallas kernels, call(): pl.pallas_call(kernel, out_shape=shapes, in_specs=[pl.BlockSpec(memory_sp...  11.8 us
    pallas_call x3, Pallas kernels, products(): pl.pallas_call(functools.partial(products_kernel, size, pieces, added is...  8.3 us
  transfers between devices with their start and end apart: 45, of which 23 were waited for; matrix products, arithmetic and copies ran while one was open for 3% of the time, Pallas kernels for 12%

profile of v1, /device:TPU:6, one launch (start us, length us, event | category | flops | bytes accessed | tf_op | source)
XLA Modules:
  0.0 144.5 jit_solution(15662076291467469995)
XLA Ops:
  0.6 1.7 %collective-permute-start.10 = (bf16[128,512]{1,0:T(8,128)(2,1)}, bf16[128,512]{1,0:T(8,128)(2,1)S(1)}, u32[]{:S(2)}, u32[]{:S(2)}) collective-permute-start(bf16[128,512]{1,0:T(8,128)(2,1)} %bitcast.26), channel_id=1, source_target_pairs={{192,0},{208,16},{224,32},{240,48},{0,64},{16,80},{32,96},{48,112}... | collective-permute-start | bytes 393224 | tf_op jit(solution)/shard_map/ppermute | solution.py:32
  2.3 2.9 %collective-permute-start.3 = (bf16[128,512]{1,0:T(8,128)(2,1)}, bf16[128,512]{1,0:T(8,128)(2,1)S(1)}, u32[]{:S(2)}, u32[]{:S(2)}) collective-permute-start(bf16[128,512]{1,0:T(8,128)(2,1)} %bitcast.27), channel_id=1, source_target_pairs={{128,0},{144,16},{160,32},{176,48},{192,64},{208,80},{224,96},{240... | collective-permute-start | bytes 393224 | tf_op jit(solution)/shard_map/ppermute | solution.py:32
  5.2 1.9 %collective-permute-start.2 = (bf16[128,512]{1,0:T(8,128)(2,1)}, bf16[128,512]{1,0:T(8,128)(2,1)S(1)}, u32[]{:S(2)}, u32[]{:S(2)}) collective-permute-start(bf16[128,512]{1,0:T(8,128)(2,1)} %bitcast.28), channel_id=1, source_target_pairs={{48,0},{0,16},{16,32},{32,48},{112,64},{64,80},{80,96},{96,112},{1... | collective-permute-start | bytes 393224 | tf_op jit(solution)/shard_map/ppermute | solution.py:32
  7.1 3.3 %collective-permute-start.1 = (bf16[128,512]{1,0:T(8,128)(2,1)}, bf16[128,512]{1,0:T(8,128)(2,1)S(1)}, u32[]{:S(2)}, u32[]{:S(2)}) collective-permute-start(bf16[128,512]{1,0:T(8,128)(2,1)} %bitcast.29), channel_id=1, source_target_pairs={{32,0},{48,16},{0,32},{16,48},{96,64},{112,80},{64,96},{80,112},{1... | collective-permute-start | bytes 393224 | tf_op jit(solution)/shard_map/ppermute | solution.py:32
  10.4 1.0 collective-permute-start
  12.0 0.7 bitcast_select_fusion
  12.7 0.7 add_bitcast_fusion
  13.4 2.2 %copy-done = bf16[1,1,128,128,128]{4,3,2,1,0:T(8,128)(2,1)S(1)} copy-done((bf16[1,1,128,128,128]{4,3,2,1,0:T(8,128)(2,1)S(1)}, bf16[1,1,128,128,128]{4,3,2,1,0:T(8,128)(2,1)}, u32[]{:S(2)}) %copy-start) | copy-done | bytes 4194328
  15.6 2.8 %shard_map.85 = (bf16[2048,896]{1,0:T(8,128)(2,1)S(1)}, bf16[2048,1152]{1,0:T(8,128)(2,1)S(1)}) custom-call(s32[2,128]{1,0:T(2,128)S(1)} %pad_add_fusion.place_ref, s32[1]{0:T(128)} %bitcast.23.count_ref, bf16[128,128,128]{2,1,0:T(8,128)(2,1)S(1)} %bitcast.24), custom_call_target="tpu_custom_call" | custom-call | bytes 12582912 | tf_op jit(solution)/shard_map/pallas_call | solution.py:100
  18.5 2.0 %collective-permute-start.9 = (bf16[128,512]{1,0:T(8,128)(2,1)S(1)}, bf16[128,512]{1,0:T(8,128)(2,1)S(1)}, u32[]{:S(2)}, u32[]{:S(2)}) collective-permute-start(bf16[128,512]{1,0:T(8,128)(2,1)S(1)} %bitcast.31), channel_id=1, source_target_pairs={{64,0},{80,16},{96,32},{112,48},{128,64},{144,80},{160,96},{176,11... | collective-permute-start | bytes 393224 | tf_op jit(solution)/shard_map/ppermute | solution.py:32
  20.6 1.4 collective-permute-start.5
  22.0 1.9 %collective-permute-start.4 = (bf16[384,512]{1,0:T(8,128)(2,1)S(1)}, bf16[384,512]{1,0:T(8,128)(2,1)S(1)}, u32[]{:S(2)}, u32[]{:S(2)}) collective-permute-start(bf16[384,512]{1,0:T(8,128)(2,1)S(1)} %get-tuple-element.157), channel_id=1, source_target_pairs={{64,0},{80,16},{96,32},{112,48},{128,64},{144,80},{160,96},{176,11... | collective-permute-start | bytes 1179656 | tf_op jit(solution)/shard_map/ppermute | solution.py:32
  23.9 1.0 collective-permute-done.9
  24.9 2.9 %collective-permute-start.7 = (bf16[128,512]{1,0:T(8,128)(2,1)S(1)}, bf16[128,512]{1,0:T(8,128)(2,1)S(1)}, u32[]{:S(2)}, u32[]{:S(2)}) collective-permute-start(bf16[128,512]{1,0:T(8,128)(2,1)S(1)} %collective-permute-done.3), channel_id=1, source_target_pairs={{48,0},{0,16},{16,32},{32,48},{112,64},{64,80},{80,96},{96,112},{1... | collective-permute-start | bytes 393224 | tf_op jit(solution)/shard_map/ppermute | solution.py:32
  27.9 1.0 collective-permute-start.6
  28.9 4.9 %shard_map.86.refs_0_ = f32[2048,512]{1,0:T(8,128)S(1)} custom-call(bf16[2048,896]{1,0:T(8,128)(2,1)S(1)} %get-tuple-element.82.dense_ref.dense1_ref, bf16[896,512]{1,0:T(8,128)(2,1)S(1)} %constant_dynamic-update-slice_fusion.3.source_ref), custom_call_target="tpu_custom_call" | custom-call | flops 1879048192 | bytes 11534336 | tf_op jit(solution)/shard_map/pallas_call | solution.py:146
  33.8 1.8 %collective-permute-done.5 = bf16[384,512]{1,0:T(8,128)(2,1)S(1)} collective-permute-done((bf16[384,512]{1,0:T(8,128)(2,1)S(1)}, bf16[384,512]{1,0:T(8,128)(2,1)S(1)}, u32[]{:S(2)}, u32[]{:S(2)}) %collective-permute-start.5) | collective-permute-done | bytes 393248 | tf_op jit(solution)/shard_map/ppermute | solution.py:32
  36.2 0.8 shard_map.87
  37.1 2.5 %shard_map.88 = f32[1536,512]{1,0:T(8,128)S(1)} custom-call(bf16[2048,1152]{1,0:T(8,128)(2,1)S(1)} %get-tuple-element.77.dense_ref.dense2_ref, bf16[1152,512]{1,0:T(8,128)(2,1)S(1)} %constant_dynamic-update-slice_fusion.10.source_ref, f32[2048,512]{1,0:T(8,128)S(1)} %shard_map.86.refs_0_), custom_call_target="tpu_custom_call" | custom-call | flops 1811939328 | bytes 10223616 | tf_op jit(solution)/shard_map/pallas_call | solution.py:146
  39.9 0.6 collective-permute-start.12
  40.7 2.0 %collective-permute-start.15 = (bf16[128,512]{1,0:T(8,128)(2,1)S(1)}, bf16[128,512]{1,0:T(8,128)(2,1)S(1)}, u32[]{:S(2)}, u32[]{:S(2)}) collective-permute-start(bf16[128,512]{1,0:T(8,128)(2,1)S(1)} %get-tuple-element.154), channel_id=1, source_target_pairs={{4,0},{5,1},{6,2},{7,3},{8,4},{9,5},{10,6},{11,7},{12,8},{13,9},{1... | collective-permute-start | bytes 393224 | tf_op jit(solution)/shard_map/ppermute | solution.py:46
  43.1 4.0 %collective-permute-done.13 = bf16[128,512]{1,0:T(8,128)(2,1)S(1)} collective-permute-done((bf16[128,512]{1,0:T(8,128)(2,1)S(1)}, bf16[128,512]{1,0:T(8,128)(2,1)S(1)}, u32[]{:S(2)}, u32[]{:S(2)}) %collective-permute-start.13) | collective-permute-done | bytes 131104 | tf_op jit(solution)/shard_map/ppermute | solution.py:46
  47.1 3.2 %collective-permute-done.15 = bf16[128,512]{1,0:T(8,128)(2,1)S(1)} collective-permute-done((bf16[128,512]{1,0:T(8,128)(2,1)S(1)}, bf16[128,512]{1,0:T(8,128)(2,1)S(1)}, u32[]{:S(2)}, u32[]{:S(2)}) %collective-permute-start.15) | collective-permute-done | bytes 131104 | tf_op jit(solution)/shard_map/ppermute | solution.py:46
  50.4 5.5 %collective-permute-start.16 = (bf16[128,512]{1,0:T(8,128)(2,1)S(1)}, bf16[128,512]{1,0:T(8,128)(2,1)S(1)}, u32[]{:S(2)}, u32[]{:S(2)}) collective-permute-start(bf16[128,512]{1,0:T(8,128)(2,1)S(1)} %add_convert_fusion.4), channel_id=1, source_target_pairs={{2,0},{3,1},{0,2},{1,3},{6,4},{7,5},{4,6},{5,7},{10,8},{11,9},{8,1... | collective-permute-start | bytes 393224 | tf_op jit(solution)/shard_map/ppermute | solution.py:46
  56.4 2.1 %collective-permute-start.18 = (bf16[128,512]{1,0:T(8,128)(2,1)S(1)}, bf16[128,512]{1,0:T(8,128)(2,1)S(1)}, u32[]{:S(2)}, u32[]{:S(2)}) collective-permute-start(bf16[128,512]{1,0:T(8,128)(2,1)S(1)} %get-tuple-element.150), channel_id=1, source_target_pairs={{8,0},{9,1},{10,2},{11,3},{12,4},{13,5},{14,6},{15,7},{0,8},{1,9},... | collective-permute-start | bytes 393224 | tf_op jit(solution)/shard_map/ppermute | solution.py:46
  58.5 2.0 %collective-permute-start.17 = (bf16[128,512]{1,0:T(8,128)(2,1)S(1)}, bf16[128,512]{1,0:T(8,128)(2,1)S(1)}, u32[]{:S(2)}, u32[]{:S(2)}) collective-permute-start(bf16[128,512]{1,0:T(8,128)(2,1)S(1)} %get-tuple-element.151), channel_id=1, source_target_pairs={{12,0},{13,1},{14,2},{15,3},{0,4},{1,5},{2,6},{3,7},{4,8},{5,9},{6... | collective-permute-start | bytes 393224 | tf_op jit(solution)/shard_map/ppermute | solution.py:46
  60.8 3.7 %collective-permute-done.19.p3 = bf16[128,512]{1,0:T(8,128)(2,1)S(1)} collective-permute-done((bf16[128,512]{1,0:T(8,128)(2,1)S(1)}, bf16[128,512]{1,0:T(8,128)(2,1)S(1)}, u32[]{:S(2)}, u32[]{:S(2)}) %collective-permute-start.19) | collective-permute-done | bytes 131104 | tf_op jit(solution)/shard_map/ppermute | solution.py:46
  65.0 1.5 %shard_map.89 = (bf16[128,512]{1,0:T(8,128)(2,1)}, bf16[1024,128]{1,0:T(8,128)(2,1)S(1)}, bf16[640,128]{1,0:T(8,128)(2,1)S(1)}, bf16[640,128]{1,0:T(8,128)(2,1)S...) custom-call(s32[2]{0:T(128)S(1)} %pad_add_fusion.1.me_ref, f32[128,512]{1,0:T(8,128)S(1)} %get-tuple-element.152.own_ref, ...), custom_call_target="tpu_custom_call" | custom-call | flops 67108864 | bytes 4194304 | tf_op jit(solution)/shard_map/pallas_call | solution.py:209
  66.6 0.8 collective-permute-start.20
  67.4 0.7 collective-permute-start.21
  68.1 2.9 %collective-permute-start.22 = (bf16[640,128]{1,0:T(8,128)(2,1)S(1)}, bf16[640,128]{1,0:T(8,128)(2,1)S(1)}, u32[]{:S(2)}, u32[]{:S(2)}) collective-permute-start(bf16[640,128]{1,0:T(8,128)(2,1)S(1)} %get-tuple-element.98), channel_id=1, source_target_pairs={{8,0},{9,1},{10,2},{11,3},{12,4},{13,5},{14,6},{15,7},{0,8},{1,9},... | collective-permute-start | bytes 491528 | tf_op jit(solution)/shard_map/ppermute | solution.py:46
  71.6 2.7 %collective-permute-done.21 = bf16[640,128]{1,0:T(8,128)(2,1)S(1)} collective-permute-done((bf16[640,128]{1,0:T(8,128)(2,1)S(1)}, bf16[640,128]{1,0:T(8,128)(2,1)S(1)}, u32[]{:S(2)}, u32[]{:S(2)}) %collective-permute-start.21) | collective-permute-done | bytes 163872 | tf_op jit(solution)/shard_map/ppermute | solution.py:46
  74.3 1.8 %collective-permute-done.22 = bf16[640,128]{1,0:T(8,128)(2,1)S(1)} collective-permute-done((bf16[640,128]{1,0:T(8,128)(2,1)S(1)}, bf16[640,128]{1,0:T(8,128)(2,1)S(1)}, u32[]{:S(2)}, u32[]{:S(2)}) %collective-permute-start.22) | collective-permute-done | bytes 163872 | tf_op jit(solution)/shard_map/ppermute | solution.py:46
  76.6 3.2 %collective-permute-done.20.both_ref = bf16[1024,128]{1,0:T(8,128)(2,1)S(1)} collective-permute-done((bf16[1024,128]{1,0:T(8,128)(2,1)S(1)}, bf16[1024,128]{1,0:T(8,128)(2,1)S(1)}, u32[]{:S(2)}, u32[]{:S(2)}) %collective-permute-start.20) | collective-permute-done | bytes 262176 | tf_op jit(solution)/shard_map/ppermute | solution.py:46
  80.0 0.6 shard_map.90
  80.7 4.0 %collective-permute-start.25 = (bf16[640,128]{1,0:T(8,128)(2,1)S(1)}, bf16[640,128]{1,0:T(8,128)(2,1)S(1)}, u32[]{:S(2)}, u32[]{:S(2)}) collective-permute-start(bf16[640,128]{1,0:T(8,128)(2,1)S(1)} %get-tuple-element.103), channel_id=1, source_target_pairs={{8,0},{9,1},{10,2},{11,3},{12,4},{13,5},{14,6},{15,7},{0,8},{1,9},... | collective-permute-start | bytes 491528 | tf_op jit(solution)/shard_map/ppermute | solution.py:46
  85.0 4.5 %shard_map.91 = (f32[512,896]{1,0:T(8,128)S(1)}, f32[512,1152]{1,0:T(8,128)S(1)}, f32[128,512]{1,0:T(8,128)S(1)}) custom-call(bf16[2048,896]{1,0:T(8,128)(2,1)S(1)} %get-tuple-element.82.dense_ref.dense1_ref, bf16[2048,1152]{1,0:T(8,128)(2,1)S(1)} %get-tuple-element.77.dense_ref.dense2_ref, bf16[640,1024]{1,0:T(8,128)(2,1)S(1)} %constant_dynamic-update-slice_fusion.15.source_ref), custom_call_target="tpu_custom_call" | custom-call | flops 2147483648 | bytes 4194304 | tf_op jit(solution)/shard_map/pallas_call | solution.py:209
  89.5 3.3 %collective-permute-done.25 = bf16[640,128]{1,0:T(8,128)(2,1)S(1)} collective-permute-done((bf16[640,128]{1,0:T(8,128)(2,1)S(1)}, bf16[640,128]{1,0:T(8,128)(2,1)S(1)}, u32[]{:S(2)}, u32[]{:S(2)}) %collective-permute-start.25) | collective-permute-done | bytes 163872 | tf_op jit(solution)/shard_map/ppermute | solution.py:46
  93.2 1.9 %collective-permute-done.28 = bf16[640,512]{1,0:T(8,128)(2,1)S(1)} collective-permute-done((bf16[640,512]{1,0:T(8,128)(2,1)S(1)}, bf16[640,512]{1,0:T(8,128)(2,1)S(1)}, u32[]{:S(2)}, u32[]{:S(2)}) %collective-permute-start.28) | collective-permute-done | bytes 655392 | tf_op jit(solution)/shard_map/ppermute | solution.py:46
  95.2 2.9 %shard_map.92 = (bf16[512,384]{1,0:T(8,128)(2,1)S(1)}, bf16[768,128]{1,0:T(8,128)(2,1)S(1)}, bf16[512,128]{1,0:T(8,128)(2,1)S(1)}, bf16[768,128]{1,0:T(8,128)(2,...) custom-call(s32[2]{0:T(128)S(1)} %pad_add_fusion.1.me_ref, ...), custom_call_target="tpu_custom_call" | custom-call | flops 1207959552 | bytes 4194304 | tf_op jit(solution)/shard_map/pallas_call | solution.py:209
  98.1 3.1 %collective-permute-start.31 = (bf16[512,384]{1,0:T(8,128)(2,1)S(1)}, bf16[512,384]{1,0:T(8,128)(2,1)S(1)}, u32[]{:S(2)}, u32[]{:S(2)}) collective-permute-start(bf16[512,384]{1,0:T(8,128)(2,1)S(1)} %get-tuple-element.125), channel_id=1, source_target_pairs={{192,0},{208,16},{224,32},{240,48},{0,64},{16,80},{32,96},{48,112}... | collective-permute-start | bytes 1179656 | tf_op jit(solution)/shard_map/ppermute | solution.py:32
  101.2 1.9 %collective-permute-start.32 = (bf16[512,384]{1,0:T(8,128)(2,1)S(1)}, bf16[512,384]{1,0:T(8,128)(2,1)S(1)}, u32[]{:S(2)}, u32[]{:S(2)}) collective-permute-start(bf16[512,384]{1,0:T(8,128)(2,1)S(1)} %get-tuple-element.126), channel_id=1, source_target_pairs={{64,0},{80,16},{96,32},{112,48},{128,64},{144,80},{160,96},{176,11... | collective-permute-start | bytes 1179656 | tf_op jit(solution)/shard_map/ppermute | solution.py:32
  103.1 1.2 collective-permute-start.30
  104.2 1.4 collective-permute-start.29
  105.6 1.3 collective-permute-start.33
  106.9 1.9 %collective-permute-done.30.w2_ref = bf16[256,128]{1,0:T(8,128)(2,1)S(1)} collective-permute-done((bf16[256,128]{1,0:T(8,128)(2,1)S(1)}, bf16[256,128]{1,0:T(8,128)(2,1)S(1)}, u32[]{:S(2)}, u32[]{:S(2)}) %collective-permute-start.30) | collective-permute-done | bytes 65568 | tf_op jit(solution)/shard_map/ppermute | solution.py:32
  108.8 2.0 %collective-permute-start.34 = (bf16[768,128]{1,0:T(8,128)(2,1)S(1)}, bf16[768,128]{1,0:T(8,128)(2,1)S(1)}, u32[]{:S(2)}, u32[]{:S(2)}) collective-permute-start(bf16[768,128]{1,0:T(8,128)(2,1)S(1)} %get-tuple-element.128), channel_id=1, source_target_pairs={{16,0},{32,16},{48,32},{0,48},{80,64},{96,80},{112,96},{64,112},{1... | collective-permute-start | bytes 589832 | tf_op jit(solution)/shard_map/ppermute | solution.py:32
  110.8 5.6 %collective-permute-done.29.across_ref = bf16[512,128]{1,0:T(8,128)(2,1)S(1)} collective-permute-done((bf16[512,128]{1,0:T(8,128)(2,1)S(1)}, bf16[512,128]{1,0:T(8,128)(2,1)S(1)}, u32[]{:S(2)}, u32[]{:S(2)}) %collective-permute-start.29) | collective-permute-done | bytes 131104 | tf_op jit(solution)/shard_map/ppermute | solution.py:32
  116.4 1.5 %shard_map.93 = (bf16[512,128]{1,0:T(8,128)(2,1)S(1)}, f32[512,128]{1,0:T(8,128)S(1)}, bf16[512,128]{1,0:T(8,128)(2,1)S(1)}, f32[512,384]{1,0:T(8,128)S(1)}, f32...) custom-call(bf16[2048,896]{1,0:T(8,128)(2,1)S(1)} %get-tuple-element.82.dense_ref.dense1_ref, ...), custom_call_target="tpu_custom_call" | custom-call | flops 939524096 | bytes 4194304 | tf_op jit(solution)/shard_map/pallas_call | solution.py:209
  118.1 1.1 collective-permute-start.35
  119.2 1.1 collective-permute-start.38
  120.4 1.9 %collective-permute-start.39 = (bf16[768,128]{1,0:T(8,128)(2,1)S(1)}, bf16[768,128]{1,0:T(8,128)(2,1)S(1)}, u32[]{:S(2)}, u32[]{:S(2)}) collective-permute-start(bf16[768,128]{1,0:T(8,128)(2,1)S(1)} %get-tuple-element.138), channel_id=1, source_target_pairs={{128,0},{144,16},{160,32},{176,48},{192,64},{208,80},{224,96},{240... | collective-permute-start | bytes 589832 | tf_op jit(solution)/shard_map/ppermute | solution.py:32
  122.3 1.1 collective-permute-start.40
  123.3 1.3 collective-permute-start.36
  124.6 0.8 collective-permute-done.35
  125.4 1.3 collective-permute-start.37
  126.7 5.5 %collective-permute-done.36 = bf16[512,128]{1,0:T(8,128)(2,1)S(1)} collective-permute-done((bf16[512,128]{1,0:T(8,128)(2,1)S(1)}, bf16[512,128]{1,0:T(8,128)(2,1)S(1)}, u32[]{:S(2)}, u32[]{:S(2)}) %collective-permute-start.36) | collective-permute-done | bytes 131104 | tf_op jit(solution)/shard_map/ppermute | solution.py:32
  132.2 2.6 %collective-permute-start.43 = (bf16[256,128]{1,0:T(8,128)(2,1)S(1)}, bf16[256,128]{1,0:T(8,128)(2,1)S(1)}, u32[]{:S(2)}, u32[]{:S(2)}) collective-permute-start(bf16[256,128]{1,0:T(8,128)(2,1)S(1)} %add_convert_fusion.10), channel_id=1, source_target_pairs={{12,0},{13,1},{14,2},{15,3},{0,4},{1,5},{2,6},{3,7},{4,8},{5,9},{6... | collective-permute-start | bytes 196616 | tf_op jit(solution)/shard_map/ppermute | solution.py:46
  134.9 0.9 collective-permute-start.41
  135.8 1.6 %collective-permute-done.43 = bf16[256,128]{1,0:T(8,128)(2,1)S(1)} collective-permute-done((bf16[256,128]{1,0:T(8,128)(2,1)S(1)}, bf16[256,128]{1,0:T(8,128)(2,1)S(1)}, u32[]{:S(2)}, u32[]{:S(2)}) %collective-permute-start.43) | collective-permute-done | bytes 65568 | tf_op jit(solution)/shard_map/ppermute | solution.py:46
  137.3 3.4 %collective-permute-done.42 = bf16[256,128]{1,0:T(8,128)(2,1)S(1)} collective-permute-done((bf16[256,128]{1,0:T(8,128)(2,1)S(1)}, bf16[256,128]{1,0:T(8,128)(2,1)S(1)}, u32[]{:S(2)}, u32[]{:S(2)}) %collective-permute-start.42) | collective-permute-done | bytes 65568 | tf_op jit(solution)/shard_map/ppermute | solution.py:46
  141.2 1.0 fusion
  142.7 0.6 shard_map.95
  143.3 1.1 convert_multiply_fusion
  (82 shorter events, 6.5 us)
Async XLA Ops:
  0.6 27.2 %collective-permute-start.10 = (bf16[128,512]{1,0:T(8,128)(2,1)}, bf16[128,512]{1,0:T(8,128)(2,1)S(1)}, u32[]{:S(2)}, u32[]{:S(2)}) collective-permute-start(bf16[128,512]{1,0:T(8,128)(2,1)} %bitcast.26), channel_id=1, source_target_pairs={{192,0},{208,16},{224,32},{240,48},{0,64},{16,80},{32,96},{48,112}... | collective-permute-start | bytes 393224 | tf_op jit(solution)/shard_map/ppermute | solution.py:32
  2.3 16.2 %collective-permute-start.3 = (bf16[128,512]{1,0:T(8,128)(2,1)}, bf16[128,512]{1,0:T(8,128)(2,1)S(1)}, u32[]{:S(2)}, u32[]{:S(2)}) collective-permute-start(bf16[128,512]{1,0:T(8,128)(2,1)} %bitcast.27), channel_id=1, source_target_pairs={{128,0},{144,16},{160,32},{176,48},{192,64},{208,80},{224,96},{240... | collective-permute-start | bytes 393224 | tf_op jit(solution)/shard_map/ppermute | solution.py:32
  5.2 15.2 %collective-permute-start.2 = (bf16[128,512]{1,0:T(8,128)(2,1)}, bf16[128,512]{1,0:T(8,128)(2,1)S(1)}, u32[]{:S(2)}, u32[]{:S(2)}) collective-permute-start(bf16[128,512]{1,0:T(8,128)(2,1)} %bitcast.28), channel_id=1, source_target_pairs={{48,0},{0,16},{16,32},{32,48},{112,64},{64,80},{80,96},{96,112},{1... | collective-permute-start | bytes 393224 | tf_op jit(solution)/shard_map/ppermute | solution.py:32
  7.1 13.3 %collective-permute-start.1 = (bf16[128,512]{1,0:T(8,128)(2,1)}, bf16[128,512]{1,0:T(8,128)(2,1)S(1)}, u32[]{:S(2)}, u32[]{:S(2)}) collective-permute-start(bf16[128,512]{1,0:T(8,128)(2,1)} %bitcast.29), channel_id=1, source_target_pairs={{32,0},{48,16},{0,32},{16,48},{96,64},{112,80},{64,96},{80,112},{1... | collective-permute-start | bytes 393224 | tf_op jit(solution)/shard_map/ppermute | solution.py:32
  10.4 10.1 %collective-permute-start = (bf16[128,512]{1,0:T(8,128)(2,1)}, bf16[128,512]{1,0:T(8,128)(2,1)S(1)}, u32[]{:S(2)}, u32[]{:S(2)}) collective-permute-start(bf16[128,512]{1,0:T(8,128)(2,1)} %bitcast.30), channel_id=1, source_target_pairs={{16,0},{32,16},{48,32},{0,48},{80,64},{96,80},{112,96},{64,112},{1... | collective-permute-start | bytes 393224 | tf_op jit(solution)/shard_map/ppermute | solution.py:32
  13.4 2.2 %copy-start = (bf16[1,1,128,128,128]{4,3,2,1,0:T(8,128)(2,1)S(1)}, bf16[1,1,128,128,128]{4,3,2,1,0:T(8,128)(2,1)}, u32[]{:S(2)}) copy-start(bf16[1,1,128,128,128]{4,3,2,1,0:T(8,128)(2,1)} %param.9) | copy-start | bytes 12582916
  15.6 2.8 %copy-start.3 = (bf16[1,128,512]{2,1,0:T(8,128)(2,1)S(1)}, bf16[1,128,512]{2,1,0:T(8,128)(2,1)}, u32[]{:S(2)}) copy-start(bf16[1,128,512]{2,1,0:T(8,128)(2,1)} %param.6) | copy-start | bytes 393220
  18.5 6.4 %collective-permute-start.9 = (bf16[128,512]{1,0:T(8,128)(2,1)S(1)}, bf16[128,512]{1,0:T(8,128)(2,1)S(1)}, u32[]{:S(2)}, u32[]{:S(2)}) collective-permute-start(bf16[128,512]{1,0:T(8,128)(2,1)S(1)} %bitcast.31), channel_id=1, source_target_pairs={{64,0},{80,16},{96,32},{112,48},{128,64},{144,80},{160,96},{176,11... | collective-permute-start | bytes 393224 | tf_op jit(solution)/shard_map/ppermute | solution.py:32
  20.4 13.4 %collective-permute-start.8 = (bf16[128,512]{1,0:T(8,128)(2,1)S(1)}, bf16[128,512]{1,0:T(8,128)(2,1)S(1)}, u32[]{:S(2)}, u32[]{:S(2)}) collective-permute-start(bf16[128,512]{1,0:T(8,128)(2,1)S(1)} %collective-permute-done.1), channel_id=1, source_target_pairs={{128,0},{144,16},{160,32},{176,48},{192,64},{208,80},{224,96},{240... | collective-permute-start | bytes 393224 | tf_op jit(solution)/shard_map/ppermute | solution.py:32
  20.6 15.0 %collective-permute-start.5 = (bf16[384,512]{1,0:T(8,128)(2,1)S(1)}, bf16[384,512]{1,0:T(8,128)(2,1)S(1)}, u32[]{:S(2)}, u32[]{:S(2)}) collective-permute-start(bf16[384,512]{1,0:T(8,128)(2,1)S(1)} %get-tuple-element.157), channel_id=1, source_target_pairs={{192,0},{208,16},{224,32},{240,48},{0,64},{16,80},{32,96},{48,112}... | collective-permute-start | bytes 1179656 | tf_op jit(solution)/shard_map/ppermute | solution.py:32
  22.0 14.1 %collective-permute-start.4 = (bf16[384,512]{1,0:T(8,128)(2,1)S(1)}, bf16[384,512]{1,0:T(8,128)(2,1)S(1)}, u32[]{:S(2)}, u32[]{:S(2)}) collective-permute-start(bf16[384,512]{1,0:T(8,128)(2,1)S(1)} %get-tuple-element.157), channel_id=1, source_target_pairs={{64,0},{80,16},{96,32},{112,48},{128,64},{144,80},{160,96},{176,11... | collective-permute-start | bytes 1179656 | tf_op jit(solution)/shard_map/ppermute | solution.py:32
  24.9 8.9 %collective-permute-start.7 = (bf16[128,512]{1,0:T(8,128)(2,1)S(1)}, bf16[128,512]{1,0:T(8,128)(2,1)S(1)}, u32[]{:S(2)}, u32[]{:S(2)}) collective-permute-start(bf16[128,512]{1,0:T(8,128)(2,1)S(1)} %collective-permute-done.3), channel_id=1, source_target_pairs={{48,0},{0,16},{16,32},{32,48},{112,64},{64,80},{80,96},{96,112},{1... | collective-permute-start | bytes 393224 | tf_op jit(solution)/shard_map/ppermute | solution.py:32
  27.9 5.9 %collective-permute-start.6 = (bf16[128,512]{1,0:T(8,128)(2,1)S(1)}, bf16[128,512]{1,0:T(8,128)(2,1)S(1)}, u32[]{:S(2)}, u32[]{:S(2)}) collective-permute-start(bf16[128,512]{1,0:T(8,128)(2,1)S(1)} %collective-permute-done.3), channel_id=1, source_target_pairs={{16,0},{32,16},{48,32},{0,48},{80,64},{96,80},{112,96},{64,112},{1... | collective-permute-start | bytes 393224 | tf_op jit(solution)/shard_map/ppermute | solution.py:32
  37.0 2.9 %collective-permute-start.11 = (bf16[512,512]{1,0:T(8,128)(2,1)S(1)}, bf16[512,512]{1,0:T(8,128)(2,1)S(1)}, u32[]{:S(2)}, u32[]{:S(2)}) collective-permute-start(bf16[512,512]{1,0:T(8,128)(2,1)S(1)} %shard_map.87), channel_id=1, source_target_pairs={{1,0},{0,1},{3,2},{2,3},{5,4},{4,5},{7,6},{6,7},{9,8},{8,9},{11,10... | collective-permute-start | bytes 1572872 | tf_op jit(solution)/shard_map/ppermute | solution.py:46
  39.9 16.0 %collective-permute-start.12 = (bf16[512,512]{1,0:T(8,128)(2,1)S(1)}, bf16[512,512]{1,0:T(8,128)(2,1)S(1)}, u32[]{:S(2)}, u32[]{:S(2)}) collective-permute-start(bf16[512,512]{1,0:T(8,128)(2,1)S(1)} %slice.152), channel_id=1, source_target_pairs={{1,0},{0,1},{3,2},{2,3},{5,4},{4,5},{7,6},{6,7},{9,8},{8,9},{11,10... | collective-permute-start | bytes 1572872 | tf_op jit(solution)/shard_map/ppermute | solution.py:46
  40.7 6.4 %collective-permute-start.13 = (bf16[128,512]{1,0:T(8,128)(2,1)S(1)}, bf16[128,512]{1,0:T(8,128)(2,1)S(1)}, u32[]{:S(2)}, u32[]{:S(2)}) collective-permute-start(bf16[128,512]{1,0:T(8,128)(2,1)S(1)} %get-tuple-element.153), channel_id=1, source_target_pairs={{12,0},{13,1},{14,2},{15,3},{0,4},{1,5},{2,6},{3,7},{4,8},{5,9},{6... | collective-permute-start | bytes 393224 | tf_op jit(solution)/shard_map/ppermute | solution.py:46
  40.7 9.5 %collective-permute-start.15 = (bf16[128,512]{1,0:T(8,128)(2,1)S(1)}, bf16[128,512]{1,0:T(8,128)(2,1)S(1)}, u32[]{:S(2)}, u32[]{:S(2)}) collective-permute-start(bf16[128,512]{1,0:T(8,128)(2,1)S(1)} %get-tuple-element.154), channel_id=1, source_target_pairs={{4,0},{5,1},{6,2},{7,3},{8,4},{9,5},{10,6},{11,7},{12,8},{13,9},{1... | collective-permute-start | bytes 393224 | tf_op jit(solution)/shard_map/ppermute | solution.py:46
  42.8 7.5 %collective-permute-start.14 = (bf16[128,512]{1,0:T(8,128)(2,1)S(1)}, bf16[128,512]{1,0:T(8,128)(2,1)S(1)}, u32[]{:S(2)}, u32[]{:S(2)}) collective-permute-start(bf16[128,512]{1,0:T(8,128)(2,1)S(1)} %get-tuple-element.155), channel_id=1, source_target_pairs={{8,0},{9,1},{10,2},{11,3},{12,4},{13,5},{14,6},{15,7},{0,8},{1,9},... | collective-permute-start | bytes 393224 | tf_op jit(solution)/shard_map/ppermute | solution.py:46
  50.3 14.7 %copy-start.1 = (bf16[512,512]{1,0:T(8,128)(2,1)S(1)}, bf16[512,512]{1,0:T(8,128)(2,1)}, u32[]{:S(2)}) copy-start(bf16[512,512]{1,0:T(8,128)(2,1)} %weight_ref.1) | copy-start | bytes 1572868
  50.4 14.7 %copy-start.2 = (bf16[1,128,512]{2,1,0:T(8,128)(2,1)S(1)}, bf16[1,128,512]{2,1,0:T(8,128)(2,1)}, u32[]{:S(2)}) copy-start(bf16[1,128,512]{2,1,0:T(8,128)(2,1)} %param.11) | copy-start | bytes 393220
  50.4 10.4 %collective-permute-start.16 = (bf16[128,512]{1,0:T(8,128)(2,1)S(1)}, bf16[128,512]{1,0:T(8,128)(2,1)S(1)}, u32[]{:S(2)}, u32[]{:S(2)}) collective-permute-start(bf16[128,512]{1,0:T(8,128)(2,1)S(1)} %add_convert_fusion.4), channel_id=1, source_target_pairs={{2,0},{3,1},{0,2},{1,3},{6,4},{7,5},{4,6},{5,7},{10,8},{11,9},{8,1... | collective-permute-start | bytes 393224 | tf_op jit(solution)/shard_map/ppermute | solution.py:46
  56.1 8.4 %collective-permute-start.19 = (bf16[128,512]{1,0:T(8,128)(2,1)S(1)}, bf16[128,512]{1,0:T(8,128)(2,1)S(1)}, u32[]{:S(2)}, u32[]{:S(2)}) collective-permute-start(bf16[128,512]{1,0:T(8,128)(2,1)S(1)} %get-tuple-element.149), channel_id=1, source_target_pairs={{4,0},{5,1},{6,2},{7,3},{8,4},{9,5},{10,6},{11,7},{12,8},{13,9},{1... | collective-permute-start | bytes 393224 | tf_op jit(solution)/shard_map/ppermute | solution.py:46
  56.4 8.1 %collective-permute-start.18 = (bf16[128,512]{1,0:T(8,128)(2,1)S(1)}, bf16[128,512]{1,0:T(8,128)(2,1)S(1)}, u32[]{:S(2)}, u32[]{:S(2)}) collective-permute-start(bf16[128,512]{1,0:T(8,128)(2,1)S(1)} %get-tuple-element.150), channel_id=1, source_target_pairs={{8,0},{9,1},{10,2},{11,3},{12,4},{13,5},{14,6},{15,7},{0,8},{1,9},... | collective-permute-start | bytes 393224 | tf_op jit(solution)/shard_map/ppermute | solution.py:46
  58.5 6.5 %collective-permute-start.17 = (bf16[128,512]{1,0:T(8,128)(2,1)S(1)}, bf16[128,512]{1,0:T(8,128)(2,1)S(1)}, u32[]{:S(2)}, u32[]{:S(2)}) collective-permute-start(bf16[128,512]{1,0:T(8,128)(2,1)S(1)} %get-tuple-element.151), channel_id=1, source_target_pairs={{12,0},{13,1},{14,2},{15,3},{0,4},{1,5},{2,6},{3,7},{4,8},{5,9},{6... | collective-permute-start | bytes 393224 | tf_op jit(solution)/shard_map/ppermute | solution.py:46
  66.6 13.2 %collective-permute-start.20 = (bf16[1024,128]{1,0:T(8,128)(2,1)S(1)}, bf16[1024,128]{1,0:T(8,128)(2,1)S(1)}, u32[]{:S(2)}, u32[]{:S(2)}) collective-permute-start(bf16[1024,128]{1,0:T(8,128)(2,1)S(1)} %get-tuple-element.96), channel_id=1, source_target_pairs={{2,0},{3,1},{0,2},{1,3},{6,4},{7,5},{4,6},{5,7},{10,8},{11,9},{8,1... | collective-permute-start | bytes 786440 | tf_op jit(solution)/shard_map/ppermute | solution.py:46
  67.4 6.9 %collective-permute-start.21 = (bf16[640,128]{1,0:T(8,128)(2,1)S(1)}, bf16[640,128]{1,0:T(8,128)(2,1)S(1)}, u32[]{:S(2)}, u32[]{:S(2)}) collective-permute-start(bf16[640,128]{1,0:T(8,128)(2,1)S(1)} %get-tuple-element.97), channel_id=1, source_target_pairs={{4,0},{5,1},{6,2},{7,3},{8,4},{9,5},{10,6},{11,7},{12,8},{13,9},{1... | collective-permute-start | bytes 491528 | tf_op jit(solution)/shard_map/ppermute | solution.py:46
  68.1 8.0 %collective-permute-start.22 = (bf16[640,128]{1,0:T(8,128)(2,1)S(1)}, bf16[640,128]{1,0:T(8,128)(2,1)S(1)}, u32[]{:S(2)}, u32[]{:S(2)}) collective-permute-start(bf16[640,128]{1,0:T(8,128)(2,1)S(1)} %get-tuple-element.98), channel_id=1, source_target_pairs={{8,0},{9,1},{10,2},{11,3},{12,4},{13,5},{14,6},{15,7},{0,8},{1,9},... | collective-permute-start | bytes 491528 | tf_op jit(solution)/shard_map/ppermute | solution.py:46
  71.0 5.6 %collective-permute-start.23 = (bf16[640,128]{1,0:T(8,128)(2,1)S(1)}, bf16[640,128]{1,0:T(8,128)(2,1)S(1)}, u32[]{:S(2)}, u32[]{:S(2)}) collective-permute-start(bf16[640,128]{1,0:T(8,128)(2,1)S(1)} %get-tuple-element.99), channel_id=1, source_target_pairs={{12,0},{13,1},{14,2},{15,3},{0,4},{1,5},{2,6},{3,7},{4,8},{5,9},{6... | collective-permute-start | bytes 491528 | tf_op jit(solution)/shard_map/ppermute | solution.py:46
  79.9 5.1 %collective-permute-start.27 = (bf16[640,512]{1,0:T(8,128)(2,1)S(1)}, bf16[640,512]{1,0:T(8,128)(2,1)S(1)}, u32[]{:S(2)}, u32[]{:S(2)}) collective-permute-start(bf16[640,512]{1,0:T(8,128)(2,1)S(1)} %pad_maximum_fusion), channel_id=1, source_target_pairs={{1,0},{0,1},{3,2},{2,3},{5,4},{4,5},{7,6},{6,7},{9,8},{8,9},{11,10... | collective-permute-start | bytes 1966088 | tf_op jit(solution)/shard_map/ppermute | solution.py:46
  80.6 8.9 %collective-permute-start.24 = (bf16[640,128]{1,0:T(8,128)(2,1)S(1)}, bf16[640,128]{1,0:T(8,128)(2,1)S(1)}, u32[]{:S(2)}, u32[]{:S(2)}) collective-permute-start(bf16[640,128]{1,0:T(8,128)(2,1)S(1)} %get-tuple-element.102), channel_id=1, source_target_pairs={{4,0},{5,1},{6,2},{7,3},{8,4},{9,5},{10,6},{11,7},{12,8},{13,9},{1... | collective-permute-start | bytes 491528 | tf_op jit(solution)/shard_map/ppermute | solution.py:46
  80.7 12.1 %collective-permute-start.25 = (bf16[640,128]{1,0:T(8,128)(2,1)S(1)}, bf16[640,128]{1,0:T(8,128)(2,1)S(1)}, u32[]{:S(2)}, u32[]{:S(2)}) collective-permute-start(bf16[640,128]{1,0:T(8,128)(2,1)S(1)} %get-tuple-element.103), channel_id=1, source_target_pairs={{8,0},{9,1},{10,2},{11,3},{12,4},{13,5},{14,6},{15,7},{0,8},{1,9},... | collective-permute-start | bytes 491528 | tf_op jit(solution)/shard_map/ppermute | solution.py:46
  84.7 8.1 %collective-permute-start.26 = (bf16[640,128]{1,0:T(8,128)(2,1)S(1)}, bf16[640,128]{1,0:T(8,128)(2,1)S(1)}, u32[]{:S(2)}, u32[]{:S(2)}) collective-permute-start(bf16[640,128]{1,0:T(8,128)(2,1)S(1)} %get-tuple-element.104), channel_id=1, source_target_pairs={{12,0},{13,1},{14,2},{15,3},{0,4},{1,5},{2,6},{3,7},{4,8},{5,9},{6... | collective-permute-start | bytes 491528 | tf_op jit(solution)/shard_map/ppermute | solution.py:46
  92.9 2.2 %collective-permute-start.28 = (bf16[640,512]{1,0:T(8,128)(2,1)S(1)}, bf16[640,512]{1,0:T(8,128)(2,1)S(1)}, u32[]{:S(2)}, u32[]{:S(2)}) collective-permute-start(bf16[640,512]{1,0:T(8,128)(2,1)S(1)} %pad_maximum_fusion.1), channel_id=1, source_target_pairs={{1,0},{0,1},{3,2},{2,3},{5,4},{4,5},{7,6},{6,7},{9,8},{8,9},{11,10... | collective-permute-start | bytes 1966088 | tf_op jit(solution)/shard_map/ppermute | solution.py:46
  98.1 19.9 %collective-permute-start.31 = (bf16[512,384]{1,0:T(8,128)(2,1)S(1)}, bf16[512,384]{1,0:T(8,128)(2,1)S(1)}, u32[]{:S(2)}, u32[]{:S(2)}) collective-permute-start(bf16[512,384]{1,0:T(8,128)(2,1)S(1)} %get-tuple-element.125), channel_id=1, source_target_pairs={{192,0},{208,16},{224,32},{240,48},{0,64},{16,80},{32,96},{48,112}... | collective-permute-start | bytes 1179656 | tf_op jit(solution)/shard_map/ppermute | solution.py:32
  101.2 16.7 %collective-permute-start.32 = (bf16[512,384]{1,0:T(8,128)(2,1)S(1)}, bf16[512,384]{1,0:T(8,128)(2,1)S(1)}, u32[]{:S(2)}, u32[]{:S(2)}) collective-permute-start(bf16[512,384]{1,0:T(8,128)(2,1)S(1)} %get-tuple-element.126), channel_id=1, source_target_pairs={{64,0},{80,16},{96,32},{112,48},{128,64},{144,80},{160,96},{176,11... | collective-permute-start | bytes 1179656 | tf_op jit(solution)/shard_map/ppermute | solution.py:32
  103.1 5.7 %collective-permute-start.30 = (bf16[256,128]{1,0:T(8,128)(2,1)S(1)}, bf16[256,128]{1,0:T(8,128)(2,1)S(1)}, u32[]{:S(2)}, u32[]{:S(2)}) collective-permute-start(bf16[256,128]{1,0:T(8,128)(2,1)S(1)} %get-tuple-element.119.w0_ref), channel_id=1, source_target_pairs={{32,0},{48,16},{0,32},{16,48},{96,64},{112,80},{64,96},{80,112},{1... | collective-permute-start | bytes 196616 | tf_op jit(solution)/shard_map/ppermute | solution.py:32
  104.2 12.1 %collective-permute-start.29 = (bf16[512,128]{1,0:T(8,128)(2,1)S(1)}, bf16[512,128]{1,0:T(8,128)(2,1)S(1)}, u32[]{:S(2)}, u32[]{:S(2)}) collective-permute-start(bf16[512,128]{1,0:T(8,128)(2,1)S(1)} %get-tuple-element.118), channel_id=1, source_target_pairs={{128,0},{144,16},{160,32},{176,48},{192,64},{208,80},{224,96},{240... | collective-permute-start | bytes 393224 | tf_op jit(solution)/shard_map/ppermute | solution.py:32
  105.6 12.2 %collective-permute-start.33 = (bf16[768,128]{1,0:T(8,128)(2,1)S(1)}, bf16[768,128]{1,0:T(8,128)(2,1)S(1)}, u32[]{:S(2)}, u32[]{:S(2)}) collective-permute-start(bf16[768,128]{1,0:T(8,128)(2,1)S(1)} %get-tuple-element.127), channel_id=1, source_target_pairs={{48,0},{0,16},{16,32},{32,48},{112,64},{64,80},{80,96},{96,112},{1... | collective-permute-start | bytes 589832 | tf_op jit(solution)/shard_map/ppermute | solution.py:32
  108.8 9.1 %collective-permute-start.34 = (bf16[768,128]{1,0:T(8,128)(2,1)S(1)}, bf16[768,128]{1,0:T(8,128)(2,1)S(1)}, u32[]{:S(2)}, u32[]{:S(2)}) collective-permute-start(bf16[768,128]{1,0:T(8,128)(2,1)S(1)} %get-tuple-element.128), channel_id=1, source_target_pairs={{16,0},{32,16},{48,32},{0,48},{80,64},{96,80},{112,96},{64,112},{1... | collective-permute-start | bytes 589832 | tf_op jit(solution)/shard_map/ppermute | solution.py:32
  118.1 7.2 %collective-permute-start.35 = (bf16[512,128]{1,0:T(8,128)(2,1)S(1)}, bf16[512,128]{1,0:T(8,128)(2,1)S(1)}, u32[]{:S(2)}, u32[]{:S(2)}) collective-permute-start(bf16[512,128]{1,0:T(8,128)(2,1)S(1)} %get-tuple-element.134), channel_id=1, source_target_pairs={{48,0},{0,16},{16,32},{32,48},{112,64},{64,80},{80,96},{96,112},{1... | collective-permute-start | bytes 393224 | tf_op jit(solution)/shard_map/ppermute | solution.py:32
  119.2 12.9 %collective-permute-start.38 = (bf16[768,128]{1,0:T(8,128)(2,1)S(1)}, bf16[768,128]{1,0:T(8,128)(2,1)S(1)}, u32[]{:S(2)}, u32[]{:S(2)}) collective-permute-start(bf16[768,128]{1,0:T(8,128)(2,1)S(1)} %get-tuple-element.137), channel_id=1, source_target_pairs={{192,0},{208,16},{224,32},{240,48},{0,64},{16,80},{32,96},{48,112}... | collective-permute-start | bytes 589832 | tf_op jit(solution)/shard_map/ppermute | solution.py:32
  120.4 11.8 %collective-permute-start.39 = (bf16[768,128]{1,0:T(8,128)(2,1)S(1)}, bf16[768,128]{1,0:T(8,128)(2,1)S(1)}, u32[]{:S(2)}, u32[]{:S(2)}) collective-permute-start(bf16[768,128]{1,0:T(8,128)(2,1)S(1)} %get-tuple-element.138), channel_id=1, source_target_pairs={{128,0},{144,16},{160,32},{176,48},{192,64},{208,80},{224,96},{240... | collective-permute-start | bytes 589832 | tf_op jit(solution)/shard_map/ppermute | solution.py:32
  122.3 9.9 %collective-permute-start.40 = (bf16[768,128]{1,0:T(8,128)(2,1)S(1)}, bf16[768,128]{1,0:T(8,128)(2,1)S(1)}, u32[]{:S(2)}, u32[]{:S(2)}) collective-permute-start(bf16[768,128]{1,0:T(8,128)(2,1)S(1)} %get-tuple-element.139), channel_id=1, source_target_pairs={{64,0},{80,16},{96,32},{112,48},{128,64},{144,80},{160,96},{176,11... | collective-permute-start | bytes 589832 | tf_op jit(solution)/shard_map/ppermute | solution.py:32
  123.3 8.8 %collective-permute-start.36 = (bf16[512,128]{1,0:T(8,128)(2,1)S(1)}, bf16[512,128]{1,0:T(8,128)(2,1)S(1)}, u32[]{:S(2)}, u32[]{:S(2)}) collective-permute-start(bf16[512,128]{1,0:T(8,128)(2,1)S(1)} %get-tuple-element.135), channel_id=1, source_target_pairs={{32,0},{48,16},{0,32},{16,48},{96,64},{112,80},{64,96},{80,112},{1... | collective-permute-start | bytes 393224 | tf_op jit(solution)/shard_map/ppermute | solution.py:32
  125.4 6.8 %collective-permute-start.37 = (bf16[512,128]{1,0:T(8,128)(2,1)S(1)}, bf16[512,128]{1,0:T(8,128)(2,1)S(1)}, u32[]{:S(2)}, u32[]{:S(2)}) collective-permute-start(bf16[512,128]{1,0:T(8,128)(2,1)S(1)} %get-tuple-element.136), channel_id=1, source_target_pairs={{16,0},{32,16},{48,32},{0,48},{80,64},{96,80},{112,96},{64,112},{1... | collective-permute-start | bytes 393224 | tf_op jit(solution)/shard_map/ppermute | solution.py:32
  132.2 5.1 %collective-permute-start.43 = (bf16[256,128]{1,0:T(8,128)(2,1)S(1)}, bf16[256,128]{1,0:T(8,128)(2,1)S(1)}, u32[]{:S(2)}, u32[]{:S(2)}) collective-permute-start(bf16[256,128]{1,0:T(8,128)(2,1)S(1)} %add_convert_fusion.10), channel_id=1, source_target_pairs={{12,0},{13,1},{14,2},{15,3},{0,4},{1,5},{2,6},{3,7},{4,8},{5,9},{6... | collective-permute-start | bytes 196616 | tf_op jit(solution)/shard_map/ppermute | solution.py:46
  134.8 5.9 %collective-permute-start.42 = (bf16[256,128]{1,0:T(8,128)(2,1)S(1)}, bf16[256,128]{1,0:T(8,128)(2,1)S(1)}, u32[]{:S(2)}, u32[]{:S(2)}) collective-permute-start(bf16[256,128]{1,0:T(8,128)(2,1)S(1)} %add_convert_fusion.10), channel_id=1, source_target_pairs={{8,0},{9,1},{10,2},{11,3},{12,4},{13,5},{14,6},{15,7},{0,8},{1,9},... | collective-permute-start | bytes 196616 | tf_op jit(solution)/shard_map/ppermute | solution.py:46
  134.9 6.2 %collective-permute-start.41 = (bf16[256,128]{1,0:T(8,128)(2,1)S(1)}, bf16[256,128]{1,0:T(8,128)(2,1)S(1)}, u32[]{:S(2)}, u32[]{:S(2)}) collective-permute-start(bf16[256,128]{1,0:T(8,128)(2,1)S(1)} %add_convert_fusion.10), channel_id=1, source_target_pairs={{4,0},{5,1},{6,2},{7,3},{8,4},{9,5},{10,6},{11,7},{12,8},{13,9},{1... | collective-permute-start | bytes 196616 | tf_op jit(solution)/shard_map/ppermute | solution.py:46
  141.1 1.6 %collective-permute-start.44 = (bf16[1024,128]{1,0:T(8,128)(2,1)S(1)}, bf16[1024,128]{1,0:T(8,128)(2,1)S(1)}, u32[]{:S(2)}, u32[]{:S(2)}) collective-permute-start(bf16[1024,128]{1,0:T(8,128)(2,1)S(1)} %pad_maximum_fusion.2.own_ref), channel_id=1, source_target_pairs={{1,0},{0,1},{3,2},{2,3},{5,4},{4,5},{7,6},{6,7},{9,8},{8,9},{11,10... | collective-permute-start | bytes 786440 | tf_op jit(solution)/shard_map/ppermute | solution.py:46
